TPU v7x, 256 devices: a whole 4x4x8 slice. The times are simulated.
256 devices in a mesh: fsdp: 32 (over y, z), tensor: 8 (over x, core).
Axes of the slice: x: 4, y: 4, z: 8, core: 2. Of those that a mesh axis runs over, the one named last changes fastest.
Arguments:
- momentum: float32 [28672, 8192], P('fsdp', 'tensor'), may hold values from -150 to 150
- gradient: bfloat16 [28672, 8192], P('fsdp', 'tensor'), may hold values from -6 to 6
- basis: bfloat16 [8192, 512], P('tensor'), may hold values from -0.0625 to 0.0625
Outputs:
- new_momentum: float32 [28672, 8192], P('fsdp', 'tensor')
- left_factor: float32 [28672, 512], P(('fsdp', 'tensor'))
- new_basis: bfloat16 [8192, 512], P('tensor')
All inputs are finite; a program needn't handle non-finite values.
Results may differ from a plain program's by a relative error of at most 0.001.
Values sent between devices are 32-bit elements; how exact they have to be, the bound alone decides.
A program may use at most 128 MiB of HBM per device.

v0:
```python
import jax
import jax.numpy as jnp
from jax import lax
from jax.sharding import PartitionSpec as P

precise = lax.Precision.HIGHEST
mu_value = 0.95
eps_value = 1e-06


def dense_nn(left_mat, right_mat):
    return jnp.dot(left_mat, right_mat, precision=precise, preferred_element_type=jnp.float32)


def dense_tn(left_mat, right_mat):
    return lax.dot_general(
        left_mat,
        right_mat,
        (((0,), (0,)), ((), ())),
        precision=precise,
        preferred_element_type=jnp.float32,
    )


def dense_nt(left_mat, right_mat):
    return lax.dot_general(
        left_mat,
        right_mat,
        (((1,), (1,)), ((), ())),
        precision=precise,
        preferred_element_type=jnp.float32,
    )


def solve_right(factor_low, matrix):
    return lax.linalg.triangular_solve(
        factor_low, matrix, left_side=False, lower=True, transpose_a=True
    )


def right_side(blended, left_full):
    partial_coef = dense_tn(blended, left_full)
    coefficients = lax.psum(partial_coef, "fsdp")
    squares = lax.psum(jnp.sum(coefficients * coefficients, axis=0), "tensor")
    return (coefficients, squares)


def body(momentum, gradient, basis):
    blended = momentum + gradient.astype(jnp.float32)
    basis_wide = basis.astype(jnp.float32)
    row_count = blended.shape[0]
    share_rows = row_count // lax.axis_size("tensor")
    tensor_pos = lax.axis_index("tensor")
    product = lax.psum(dense_nn(blended, basis_wide), "tensor")
    gram = lax.psum(dense_tn(product, product), "fsdp")
    factor_low = jnp.linalg.cholesky(gram)
    left_full = solve_right(factor_low, product)
    own_left = lax.dynamic_slice_in_dim(left_full, tensor_pos * share_rows, share_rows, 0)
    coefficients, squares = right_side(blended, left_full)
    col_norms = jnp.sqrt(squares + eps_value)
    new_basis = (coefficients / col_norms[None, :]).astype(jnp.bfloat16)
    new_momentum = blended - (1.0 - mu_value) * dense_nt(left_full, coefficients)
    return (new_momentum, own_left, new_basis)


def solution(mesh):
    placed = (P("fsdp", "tensor"), P("fsdp", "tensor"), P("tensor", None))
    return jax.shard_map(
        body,
        mesh=mesh,
        in_specs=placed,
        out_specs=(P("fsdp", "tensor"), P(("fsdp", "tensor"), None), P("tensor", None)),
        check_vma=False,
    )
```

profile of v0, /device:TPU:1, one launch (start us, length us, event | category | flops | bytes accessed | tf_op | source)
XLA Modules:
  0.0 609.4 jit_solution(16759321625143815848)
XLA Ops:
  7.2 1.2 copy-done
  8.4 6.9 %fusion.1 = f32[896,512]{1,0:T(8,128)} fusion(bf16[1024,512]{1,0:T(8,128)(2,1)S(1)} %copy-done, f32[896,1024]{1,0:T(8,128)} %param.3, bf16[896,1024]{1,0:T(8,128)(2,1)} %param.4), kind=kOutput, calls=%fused_computation.8 | convolution fusion | flops 5638979584 | bytes 8388608 | tf_op jit(solution)/shard_map/dot_general | solution.py:12
  15.3 71.9 %all-reduce.5.cloned.1.call-done = f32[896,512]{1,0:T(8,128)} async-done(((f32[896,512]{1,0:T(8,128)}), f32[896,512]{1,0:T(8,128)}) %all-reduce.5.cloned.1.call-update) | async-done | bytes 1835024 | tf_op jit(solution)/shard_map/psum | solution.py:54
  87.2 6.5 %fusion.37 = f32[512,512]{0,1:T(8,128)} fusion(f32[896,512]{1,0:T(8,128)} %all-reduce.5.cloned.1.call-done), kind=kOutput, calls=%fused_computation.76 | convolution fusion | flops 2818572288 | bytes 2883584 | tf_op jit(solution)/shard_map/dot_general | solution.py:16
  94.1 146.3 %all-reduce.7.cloned.1.call-done = f32[512,512]{0,1:T(8,128)} async-done(((f32[512,512]{0,1:T(8,128)}), f32[512,512]{0,1:T(8,128)}) %all-reduce.7.cloned.1.call-update) | async-done | bytes 1048592 | tf_op jit(solution)/shard_map/psum | solution.py:55
  240.4 1.6 copy.7
  242.3 1.0 copy-done.10
  243.3 11.7 %cholesky.104 = f32[128,128]{1,0:T(8,128)S(1)} custom-call(f32[128,128]{1,0:T(8,128)S(1)} %cholesky.266), custom_call_target="Cholesky" | custom-call | tf_op jit(solution)/shard_map/jit(cholesky)/cholesky | solution.py:56
  255.0 9.8 %custom-call.30 = f32[1,128,128]{1,2,0:T(8,128)S(1)} custom-call(f32[1,128,128]{2,1,0:T(8,128)S(1)} %get-tuple-element.33), custom_call_target="InvertDiagBlocksLowerTriangular" | custom-call | tf_op jit(solution)/shard_map/jit(cholesky)/cholesky | solution.py:56
  264.9 1.1 cholesky.224
  266.0 1.9 constant_dynamic-update-slice_fusion.3
  267.9 1.2 convolution_subtract_fusion.2
  269.1 11.7 %cholesky.217 = f32[128,128]{1,0:T(8,128)S(1)} custom-call(f32[128,128]{1,0:T(8,128)S(1)} %cholesky.270), custom_call_target="Cholesky" | custom-call | tf_op jit(solution)/shard_map/jit(cholesky)/cholesky | solution.py:56
  280.8 0.6 select_reduce_fusion.2
  281.5 10.2 %custom-call.31 = f32[1,128,128]{1,2,0:T(8,128)S(1)} custom-call(f32[1,128,128]{2,1,0:T(8,128)S(1)} %get-tuple-element.30), custom_call_target="InvertDiagBlocksLowerTriangular" | custom-call | tf_op jit(solution)/shard_map/jit(cholesky)/cholesky | solution.py:56
  291.7 0.9 convolution_dynamic-update-slice_fusion
  292.6 1.4 convolution_subtract_fusion.3
  294.0 11.7 %cholesky.238 = f32[128,128]{1,0:T(8,128)S(1)} custom-call(f32[128,128]{1,0:T(8,128)S(1)} %cholesky.275), custom_call_target="Cholesky" | custom-call | tf_op jit(solution)/shard_map/jit(cholesky)/cholesky | solution.py:56
  305.7 0.6 select_reduce_fusion.1
  306.4 0.6 compare_reduce_fusion.1
  307.0 9.8 %custom-call.32 = f32[1,128,128]{1,2,0:T(8,128)S(1)} custom-call(f32[1,128,128]{2,1,0:T(8,128)S(1)} %get-tuple-element.27), custom_call_target="InvertDiagBlocksLowerTriangular" | custom-call | tf_op jit(solution)/shard_map/jit(cholesky)/cholesky | solution.py:56
  316.8 0.8 convolution_dynamic-update-slice_fusion.1
  317.7 1.4 convolution_subtract_fusion.4
  319.1 11.7 %cholesky.255 = f32[128,128]{1,0:T(8,128)S(1)} custom-call(f32[128,128]{1,0:T(8,128)S(1)} %convolution_subtract_fusion.4), custom_call_target="Cholesky" | custom-call | tf_op jit(solution)/shard_map/jit(cholesky)/cholesky | solution.py:56
  330.8 0.6 select_reduce_fusion
  331.5 0.7 compare_reduce_fusion
  332.2 0.7 compare_reduce_fusion.2
  335.5 2.5 select_select_fusion
  338.0 11.3 %while.1 = (s32[]{:T(128)}, f32[512,512]{1,0:T(8,128)}, s32[4,2]{0,1:T(2,128)S(1)}, f32[4,128,128]{2,1,0:T(8,128)S(1)}, s32[]{:T(128)}) while((s32[]{:T(128)}, f32[512,512]{1,0:T(8,128)}, s32[4,2]{0,1:T(2,128)S(1)}, f32[4,128,128]{2,1,0:T(8,128)S(1)}, s32[]{:T(128)}) %tuple.32), condition=%wide.while_cond, body=%wide.while_body.sunk | while | flops 2 | bytes 131189 | solution.py:36
  338.6 2.2 bitcast_dynamic-update-slice_fusion.2
  341.4 2.2 bitcast_dynamic-update-slice_fusion.2
  344.3 2.2 bitcast_dynamic-update-slice_fusion.2
  347.1 2.2 bitcast_dynamic-update-slice_fusion.2
  349.3 39.9 %custom-call.33 = f32[4,128,128]{1,2,0:T(8,128)} custom-call(f32[4,128,128]{2,1,0:T(8,128)S(1)} %get-tuple-element.10), custom_call_target="InvertDiagBlocksLowerTriangular" | custom-call | tf_op jit(solution)/shard_map/triangular_solve | solution.py:36
  389.2 1.6 fusion.15
  390.8 1.7 convolution_subtract_fusion.1
  393.2 2.7 convolution_subtract_fusion
  396.6 3.8 fusion.8
  401.1 0.8 copy-done.8
  401.9 13.2 %fusion = f32[1024,512]{1,0:T(8,128)} fusion(f32[896,1024]{1,0:T(8,128)S(1)} %copy-done.1, bf16[896,1024]{1,0:T(8,128)(2,1)S(1)} %copy-done.2, f32[896,128]{0,1:T(8,128)S(1)} %fusion.25, f32[896,128]{0,1:T(8,128)S(1)} %fusion.26, f32[896,128]{0,1:T(8,128)S(1)} %fusion.27, f32[896,128]{0,1:T(8,128)S(1)} %fusion.15), kind=kOutput, calls=%fused_computation.7 | convolution fusion | flops 5640355840 | bytes 9437184 | tf_op jit(solution)/shard_map/dot_general | solution.py:16
  415.1 1.4 pad_maximum_fusion
  416.5 0.9 constant_dynamic-slice_fusion.1
  417.4 1.8 copy.8
  419.2 147.8 %all-reduce.9.cloned.1.call-done = f32[1024,512]{1,0:T(8,128)} async-done(((f32[1024,512]{1,0:T(8,128)}), f32[1024,512]{1,0:T(8,128)}) %all-reduce.9.cloned.1.call-update) | async-done | bytes 2097168 | tf_op jit(solution)/shard_map/psum | solution.py:43
  567.0 1.8 multiply_reduce_fusion
  568.8 17.2 %psum.31 = f32[512]{0:T(512)S(1)} all-reduce(f32[512]{0:T(512)S(1)} %multiply_reduce_fusion), channel_id=1, replica_groups=mesh['fsdp'=32,'tensor'=8] {'tensor'}, use_global_device_ids=true, to_apply=%region_12.13 | all-reduce | flops 512 | bytes 4096 | tf_op jit(solution)/shard_map/psum | solution.py:44
  586.0 15.4 %multiply_subtract_fusion = f32[896,1024]{1,0:T(8,128)} fusion(f32[1024,512]{1,0:T(8,128)} %all-reduce.9.cloned.1.call-done, f32[896,1024]{1,0:T(8,128)} %param.3, bf16[896,1024]{1,0:T(8,128)(2,1)S(1)} %copy-done.2, f32[896,128]{0,1:T(8,128)} %copy-done.8, f32[896,128]{0,1:T(8,128)} %copy-done.7, f32[896,128]{0,1:T(8,128)} %copy-done.6, ...), kind=kOutput, calls=%fused_computation.2 | convolution fusion | flops 5642190848 | bytes 13107200 | tf_op jit(solution)/shard_map/dot_general | solution.py:26
  601.4 1.2 divide_convert_fusion
  (47 shorter events, 4.9 us)
Async XLA Ops:
  7.2 1.2 copy-start
  7.2 80.1 %all-reduce.5.cloned.1.call-start = ((), (), s32[]{:S(2)}) async-start(), calls=%async_computation | async-start | bytes 3670016 | tf_op jit(solution)/shard_map/psum | solution.py:54
  15.3 225.1 %all-reduce.7.cloned.1.call-start = ((), (), s32[]{:S(2)}) async-start(), calls=%async_computation.1 | async-start | bytes 2097152 | tf_op jit(solution)/shard_map/psum | solution.py:55
  93.8 473.2 %all-reduce.9.cloned.1.call-start = ((), (), s32[]{:S(2)}) async-start(), calls=%async_computation.2 | async-start | bytes 4194304 | tf_op jit(solution)/shard_map/psum | solution.py:43
  240.4 1.7 copy-start.9
  242.3 1.0 copy-start.10
  306.4 82.8 %copy-start.4 = (f32[896,512]{1,0:T(8,128)S(1)}, f32[896,512]{1,0:T(8,128)}, u32[]{:S(2)}) copy-start(f32[896,512]{1,0:T(8,128)} %all-reduce.5.cloned.1.call-done) | copy-start | bytes 5505028
  389.2 3.4 copy-start.11
  389.2 4.0 copy-start.5
  393.2 7.9 %copy-start.6 = (f32[896,128]{0,1:T(8,128)}, f32[896,128]{0,1:T(8,128)S(1)}, u32[]{:S(2)}) copy-start(f32[896,128]{0,1:T(8,128)S(1)} %fusion.27) | copy-start | bytes 1376260
  393.2 8.6 %copy-start.2 = (bf16[896,1024]{1,0:T(8,128)(2,1)S(1)}, bf16[896,1024]{1,0:T(8,128)(2,1)}, u32[]{:S(2)}) copy-start(bf16[896,1024]{1,0:T(8,128)(2,1)} %param.4) | copy-start | bytes 5505028
  396.0 5.9 copy-start.1
  396.6 4.5 copy-start.7
  401.1 0.8 copy-start.8
  586.0 15.4 %copy-start.3 = (f32[1024,512]{1,0:T(8,128)S(1)}, f32[1024,512]{1,0:T(8,128)}, u32[]{:S(2)}) copy-start(f32[1024,512]{1,0:T(8,128)} %all-reduce.9.cloned.1.call-done) | copy-start | bytes 6291460
Sparse Core Ops, SparseCore 0:
  15.4 71.8 all-reduce.4
  93.9 146.4 all-reduce.6
  415.2 151.7 all-reduce.8
where the time goes:
time: 615 us; the launch traced here: 609 us
  waiting for transfers between devices  366 us (60%)
  other arithmetic  128 us (21%)
  matrix products  61.5 us (10%)
  local copies, waits for them, and re-layouts  19.6 us (3%)
  blocking collectives  17.2 us (3%)
  between operations  16.9 us (3%)
    psum x1, waiting for transfers between devices, right_side(): coefficients = lax.psum(partial_coef, 'fsdp')  148 us
    psum x1, waiting for transfers between devices, body(): gram = lax.psum(dense_tn(product, product), 'fsdp')  146 us
    another operation x14, other arithmetic, body(): factor_low = jnp.linalg.cholesky(gram)  80.7 us
    psum x1, waiting for transfers between devices, body(): product = lax.psum(dense_nn(blended, basis_wide), 'tensor')  71.9 us
    another operation x4, other arithmetic, solve_right(): lax.linalg.triangular_solve(factor_low, matrix, left_side=False, lower=Tr...  43.9 us
    dot_general x2, matrix products, dense_tn(): lax.dot_general(left_mat, right_mat, (((0,), (0,)), ((), ())), precision=...  19.7 us
    psum x1, blocking collectives, right_side(): squares = lax.psum(jnp.sum(coefficients * coefficients, axis=0), 'tensor')  17.2 us
    dot_general x1, matrix products, dense_nt(): lax.dot_general(left_mat, right_mat, (((1,), (1,)), ((), ())), precision=...  15.4 us
  transfers between devices with their start and end apart: 3, of which 3 were waited for; matrix products, arithmetic and copies ran while one was open for 1% of the time, Pallas kernels for 0%

commit v1 on v0

v1 whole, which is shorter than its diff:
```python
import functools

import jax
import jax.numpy as jnp
from jax import lax
from jax.experimental import pallas as pl
from jax.experimental.pallas import tpu as pltpu
from jax.sharding import PartitionSpec as P

mu_value = 0.95
eps_value = 1e-06
f32 = jnp.float32
bf16 = jnp.bfloat16
MESH = pl.DeviceIdType.MESH
HIGHEST = lax.Precision.HIGHEST
NB = 128


def dot(left, right, dims=((1,), (0,)), precision=None):
    return lax.dot_general(left, right, (dims, ((), ())), precision=precision, preferred_element_type=f32)


def exact_dot(left, right, dims=((1,), (0,))):
    return dot(left, right, dims, HIGHEST)


def split2(value):
    high = value.astype(bf16)
    return high, (value - high.astype(f32)).astype(bf16)


def dot3(left, right, dims=((1,), (0,))):
    left_high, left_low = left
    right_high, right_low = right
    return dot(left_high, right_high, dims) + (dot(left_low, right_high, dims) + dot(left_high, right_low, dims))


def factor_groups(work, inverse, first, last):
    for group in range(first, last):
        r0 = 8 * group
        n = NB - r0
        cols = [jnp.broadcast_to(work[r0:NB, r0 + j : r0 + j + 1], (n, 128)) for j in range(8)]
        top = work[r0 : r0 + 8, :]
        rows = []
        for k in range(8):
            inv = lax.rsqrt(cols[k][k : k + 1, :])
            c = cols[k] * inv
            cols[k] = c
            for j in range(k + 1, 8):
                cols[j] = cols[j] - c * c[j : j + 1, :]
            row = top[k : k + 1, :] * jnp.concatenate([inv, inv], axis=1)
            rows.append(row)
            if k < 7:
                top = top - jnp.concatenate([c[0:8], c[0:8]], axis=1) * row
            inverse[r0 + k : r0 + k + 1, :] = row[:, 128:]
        if n > 8:
            for half in (slice(0, 128), slice(128, 256)):
                rest = work[r0 + 8 : NB, half]
                for k in range(8):
                    rest = rest - cols[k][8:] * rows[k][:, half]
                work[r0 + 8 : NB, half] = rest


class Links:
    def __init__(self, dims, send_sems, recv_sems):
        self.nx, self.ny, self.nz = dims
        f, t = lax.axis_index("fsdp"), lax.axis_index("tensor")
        self.y, self.z = f // self.nz, lax.rem(f, self.nz)
        self.x, self.c = t // 2, lax.rem(t, 2)
        self.t, self.f = t, f
        self.send_sems, self.recv_sems = send_sems, recv_sems
        self.count = 0
        self.sent = []

    def size(self, axis):
        return {"x": self.nx, "y": self.ny, "z": self.nz}[axis]

    def pos(self, axis):
        return {"x": self.x, "y": self.y, "z": self.z}[axis]

    def at(self, axis, offset):
        n = self.size(axis)
        return lax.rem(self.pos(axis) + (offset % n), n)

    def device(self, dx=0, dy=0, dz=0, core=0):
        x, y, z = self.at("x", dx), self.at("y", dy), self.at("z", dz)
        c = 1 - self.c if core else self.c
        return (y * self.nz + z, x * 2 + c)

    def along(self, axis, offset):
        return self.device(**{"d" + axis: offset})

    def send(self, src, dst, device):
        number = self.count
        self.count += 1
        copy = pltpu.make_async_remote_copy(
            src_ref=src,
            dst_ref=dst,
            send_sem=self.send_sems.at[number],
            recv_sem=self.recv_sems.at[number],
            device_id=device,
            device_id_type=MESH,
        )
        copy.start()
        self.sent.append(copy)
        return number

    def wait(self, number, landing):
        pltpu.make_async_remote_copy(
            src_ref=landing,
            dst_ref=landing,
            send_sem=self.send_sems.at[number],
            recv_sem=self.recv_sems.at[number],
            device_id=self.device(core=1),
            device_id_type=MESH,
        ).wait_recv()


def halves(width):
    return (slice(0, width // 2), slice(width // 2, width))


def reduce_ring(links, axis, block, plus, minus, width):
    n = links.size(axis)
    half = n // 2
    first, second = halves(width)
    state = {}

    def add(target, slot, cols):
        target[:, cols] = target[:, cols] + slot[:, cols]

    def step(s):
        k = half + 1 - s
        ahead, behind = block(links.at(axis, k)), block(links.at(axis, -k))
        if s > 1:
            cols_a = first if s == 2 else slice(0, width)
            cols_b = second if s == 2 else slice(0, width)
            links.wait(state["plus"], plus.at[s - 2, :, cols_a])
            add(ahead, plus.at[s - 2], cols_a)
        cols_a = first if s == 1 else slice(0, width)
        state["plus"] = links.send(ahead.at[:, cols_a], plus.at[s - 1, :, cols_a], links.along(axis, 1))
        if s > 1:
            links.wait(state["minus"], minus.at[s - 2, :, cols_b])
            add(behind, minus.at[s - 2], cols_b)
        cols_b = second if s == 1 else slice(0, width)
        state["minus"] = links.send(behind.at[:, cols_b], minus.at[s - 1, :, cols_b], links.along(axis, -1))

    def last():
        own = block(links.pos(axis))
        cols_a = first if half == 1 else slice(0, width)
        cols_b = second if half == 1 else slice(0, width)
        links.wait(state["plus"], plus.at[half - 1, :, cols_a])
        add(own, plus.at[half - 1], cols_a)
        links.wait(state["minus"], minus.at[half - 1, :, cols_b])
        add(own, minus.at[half - 1], cols_b)

    return [functools.partial(step, s) for s in range(1, half + 1)] + [last]


def gather_ring(links, axis, block, cut, on_block=None):
    n = links.size(axis)
    half = n // 2
    state = {}

    def step(s):
        ahead, behind = block(links.at(axis, 1 - s)), block(links.at(axis, s - 1))
        if s > 1:
            links.wait(state["plus"], ahead)
        view = cut(ahead)[0] if s == half else ahead
        state["plus"] = links.send(view, view, links.along(axis, 1))
        if s > 1:
            links.wait(state["minus"], behind)
        view = cut(behind)[1] if s == half else behind
        state["minus"] = links.send(view, view, links.along(axis, -1))
        if on_block is not None:
            on_block(links.at(axis, 1 - s))
            if s > 1:
                on_block(links.at(axis, s - 1))

    def last():
        far = cut(block(links.at(axis, half)))
        links.wait(state["plus"], far[0])
        links.wait(state["minus"], far[1])
        if on_block is not None:
            on_block(links.at(axis, half))

    return [functools.partial(step, s) for s in range(1, half + 1)] + [last]


def cut_columns(view):
    width = view.shape[1]
    return view.at[:, 0 : width // 2], view.at[:, width // 2 : width]


def cut_rows(view):
    size = view.shape[0]
    return view.at[0 : size // 2], view.at[size // 2 : size]


def kernel(
    dims,
    mom_hbm, grad_hbm, basis_hbm,
    out_hbm, left_hbm, newb_hbm,
    blend, grad, basis, blend_hi, blend_lo, part, from_core, x_plus, x_minus,
    full, flip, flip_hi, flip_lo,
    piece, from_y, from_z, tiles, gram_all, sym, low, work, diag_inv, inverse,
    wide, ay_plus, ay_minus, az_plus, az_minus, bz_plus, bz_minus, by_plus, by_minus, wide_all,
    coef_t, coef, squares, left_bf, left_own, newb,
    load_sems, store_sems, send_sems, recv_sems,
):
    nx, ny, nz = dims
    nt = 2 * nx
    rows, width = blend.shape
    rank = basis.shape[1]
    share = rows // nt
    links = Links(dims, send_sems, recv_sems)
    chip_rows = 2 * share

    loads = []
    basis_copy = pltpu.make_async_copy(basis_hbm, basis, load_sems.at[2 * nx])
    basis_copy.start()
    for k in range(nx):
        chip = links.at("x", [nx // 2, 1, nx - 1, 0][k] if nx == 4 else k + 1)
        span = pl.ds(pl.multiple_of(chip * chip_rows, chip_rows), chip_rows)
        m = pltpu.make_async_copy(mom_hbm.at[span], blend.at[span], load_sems.at[2 * k])
        g = pltpu.make_async_copy(grad_hbm.at[span], grad.at[span], load_sems.at[2 * k + 1])
        m.start()
        g.start()
        loads.append((m, g, span, chip))

    barrier = pltpu.get_barrier_semaphore()
    peers = [links.device(core=1)]
    peers += [links.device(dx=d, core=c) for d in range(1, nx) for c in (0, 1)]
    peers += [links.along("y", d) for d in range(1, ny)]
    peers += [links.along("z", d) for d in range(1, nz)]
    for peer in peers:
        pl.semaphore_signal(barrier, inc=1, device_id=peer, device_id_type=MESH)
    pl.semaphore_wait(barrier, len(peers))

    def share_of(ref, chip, core):
        return ref.at[pl.ds(pl.multiple_of((2 * chip + core) * share, share), share)]

    basis_copy.wait()
    core_numbers = []
    for m, g, span, chip in loads:
        m.wait()
        g.wait()
        value = blend[span] + grad[span].astype(f32)
        blend[span] = value
        high = value.astype(bf16)
        rest = value - high.astype(f32)
        mid = rest.astype(bf16)
        tail = (rest - mid.astype(f32)).astype(bf16)
        blend_hi[span] = high
        blend_lo[span] = mid
        q = basis[...]
        part[span] = dot(high, q) + (dot(mid, q) + dot(tail, q))
        number = links.send(
            share_of(part, chip, 1 - links.c), from_core.at[pl.ds(chip * share, share)], links.device(core=1)
        )
        core_numbers.append((number, chip))
    for number, chip in core_numbers:
        landing = from_core.at[pl.ds(chip * share, share)]
        links.wait(number, landing)
        mine = share_of(part, chip, links.c)
        mine[...] = mine[...] + landing[...]

    for step in reduce_ring(links, "x", lambda i: share_of(part, i, links.c), x_plus, x_minus, rank):
        step()
    own = share_of(part, links.x, links.c)
    share_of(full, links.x, links.c)[...] = own[...]

    def gather_tensor(view, cut):
        numbers = []

        def to_core(chip):
            numbers.append((links.send(view(chip, links.c), view(chip, links.c), links.device(core=1)), chip))

        def finish():
            for number, chip in numbers:
                links.wait(number, view(chip, 1 - links.c))

        return gather_ring(links, "x", lambda i: view(i, links.c), cut, to_core) + [finish]

    for step in gather_tensor(functools.partial(share_of, full), cut_columns):
        step()

    for i in range(rows // 128):
        for j in range(rank // 128):
            block = full[128 * i : 128 * i + 128, 128 * j : 128 * j + 128].T
            flip[128 * j : 128 * j + 128, 128 * i : 128 * i + 128] = block
            high, lower = split2(block)
            flip_hi[128 * j : 128 * j + 128, 128 * i : 128 * i + 128] = high
            flip_lo[128 * j : 128 * j + 128, 128 * i : 128 * i + 128] = lower

    nb = rank // NB
    fine = NB // nt
    picked = jnp.concatenate(
        [flip[pl.ds(pl.multiple_of(NB * i + fine * links.t, 8), fine), :] for i in range(nb)], axis=0
    )
    strip = exact_dot(picked, full[...])
    blocks = [(i, j) for i in range(nb) for j in range(i, nb)]
    per = fine // 8
    for b, (i, j) in enumerate(blocks):
        piece[b * fine : b * fine + fine, :] = strip[i * fine : i * fine + fine, NB * j : NB * j + NB]
    piece_rows = len(blocks) * fine
    y_rows = piece_rows // ny

    def y_view(ref, i):
        return ref.at[pl.ds(pl.multiple_of(i * y_rows, 8), y_rows)]

    y_numbers = [
        links.send(y_view(piece, links.at("y", d)), from_y.at[d - 1], links.along("y", d)) for d in range(1, ny)
    ]

    def wide_part(h):
        span = slice(h * (rank // 2), (h + 1) * (rank // 2))
        for j in range(width // 256):
            cols = slice(256 * j, 256 * j + 256)
            wide[span, cols] = dot3((flip_hi[span, :], flip_lo[span, :]), (blend_hi[:, cols], blend_lo[:, cols]))

    wide_part(0)
    total = y_view(piece, links.y)[...]
    for d, number in zip(range(1, ny), y_numbers):
        links.wait(number, from_y.at[d - 1])
        total = total + from_y[d - 1]
    from_z[links.z] = total
    z_numbers = [
        links.send(from_z.at[links.z], from_z.at[links.z], links.along("z", d)) for d in range(1, nz)
    ]
    wide_part(1)
    for d, number in zip(range(1, nz), z_numbers):
        links.wait(number, from_z.at[links.at("z", -d)])
    total = from_z[0]
    for i in range(1, nz):
        total = total + from_z[i]
    mine = gram_all.at[links.t]
    y_view(mine, links.y)[...] = total
    y_numbers = [
        links.send(y_view(mine, links.y), y_view(mine, links.y), links.along("y", d)) for d in range(1, ny)
    ]

    half = rank // 2
    ay, az = half // ny, half // ny // nz
    bz, by = half // nz, half // nz // ny
    start_az = links.y * ay
    start_bz = half + links.z * bz

    def rows_of(ref, start, size):
        return ref.at[pl.ds(pl.multiple_of(start, 8), size)]

    def copy_out_a():
        rows_of(wide_all, start_az + links.z * az, az)[...] = rows_of(wide, start_az + links.z * az, az)[...]

    def copy_out_b():
        rows_of(wide_all, start_bz + links.y * by, by)[...] = rows_of(wide, start_bz + links.y * by, by)[...]

    hooks_a = (
        reduce_ring(links, "y", lambda i: rows_of(wide, i * ay, ay), ay_plus, ay_minus, width)
        + reduce_ring(links, "z", lambda i: rows_of(wide, start_az + i * az, az), az_plus, az_minus, width)
        + [copy_out_a]
        + gather_ring(links, "z", lambda i: rows_of(wide_all, start_az + i * az, az), cut_columns)
        + gather_ring(links, "y", lambda i: rows_of(wide_all, i * ay, ay), cut_columns)
    )
    hooks_b = (
        reduce_ring(links, "z", lambda i: rows_of(wide, half + i * bz, bz), bz_plus, bz_minus, width)
        + reduce_ring(links, "y", lambda i: rows_of(wide, start_bz + i * by, by), by_plus, by_minus, width)
        + [copy_out_b]
        + gather_ring(links, "y", lambda i: rows_of(wide_all, start_bz + i * by, by), cut_columns)
        + gather_ring(links, "z", lambda i: rows_of(wide_all, half + i * bz, bz), cut_columns)
    )
    hooks = []
    for a, b in zip(hooks_a, hooks_b):
        hooks += [b, a]
    assert len(hooks_a) == len(hooks_b)
    hooks.reverse()

    def serve(count):
        for _ in range(count):
            if hooks:
                hooks.pop()()

    for d, number in zip(range(1, ny), y_numbers):
        links.wait(number, y_view(mine, links.at("y", -d)))
    serve(2)
    for step in gather_tensor(lambda chip, core: gram_all.at[2 * chip + core], cut_rows):
        step()
    for b, (i, j) in enumerate(blocks):
        for s in range(nt):
            sym[NB * i + fine * s : NB * i + fine * s + fine, NB * j : NB * j + NB] = gram_all[
                s, b * fine : b * fine + fine, :
            ]

    eye = jnp.where(
        lax.broadcasted_iota(jnp.int32, (NB, NB), 0) == lax.broadcasted_iota(jnp.int32, (NB, NB), 1), 1.0, 0.0
    ).astype(f32)
    low[...] = jnp.zeros_like(low)
    inverse[...] = jnp.zeros_like(inverse)
    for k in range(nb):
        s = slice(NB * k, NB * k + NB)
        work[:, :NB] = sym[s, s]
        work[:, NB:] = eye
        for g in range(0, 16, 4):
            factor_groups(work, diag_inv, g, g + 4)
            serve(2)
        block_inv = diag_inv[...]
        inverse[s, s] = block_inv
        if k:
            inverse[s, 0 : NB * k] = exact_dot(block_inv, low[s, 0 : NB * k])
        if k < nb - 1:
            upper = exact_dot(block_inv, sym[s, NB * k + NB :])
            for i in range(k + 1, nb):
                column = upper[:, NB * (i - k - 1) : NB * (i - k)]
                sym[NB * i : NB * i + NB, NB * i :] -= exact_dot(
                    column, upper[:, NB * (i - k - 1) :], ((0,), (0,))
                )
            low[NB * k + NB :, 0 : NB * k + NB] -= exact_dot(upper, inverse[s, 0 : NB * k + NB], ((0,), (0,)))
        serve(1)
    serve(len(hooks))

    inverse_parts = split2(inverse[...])
    left_own[...] = exact_dot(share_of(full, links.x, links.c)[...], inverse[...], ((1,), (1,)))
    left_copy = pltpu.make_async_copy(left_own, left_hbm, store_sems.at[0])
    left_copy.start()
    for j in range(width // 256):
        cols = slice(256 * j, 256 * j + 256)
        block = dot3(inverse_parts, split2(wide_all[:, cols]))
        coef_t[:, cols] = ((mu_value - 1.0) * block).astype(bf16)
        for q in range(2):
            for r in range(rank // 128):
                coef[256 * j + 128 * q : 256 * j + 128 * q + 128, 128 * r : 128 * r + 128] = block[
                    128 * r : 128 * r + 128, 128 * q : 128 * q + 128
                ].T
    value = coef[...]
    mine = squares.at[links.t]
    mine[...] = jnp.broadcast_to(jnp.sum(value * value, axis=0, keepdims=True), (8, rank))
    numbers = []
    for d in range(nx):
        for core in (0, 1):
            if d or core:
                other = 2 * links.at("x", -d) + (1 - links.c if core else links.c)
                numbers.append((links.send(mine, mine, links.device(dx=d, core=core)), other))
    stores = []
    step_rows = rows // nx
    for k in range(nx):
        span = slice(k * step_rows, (k + 1) * step_rows)
        left_bf[span] = dot3(split2(full[span]), inverse_parts, ((1,), (1,))).astype(bf16)
        blend[span] = blend[span] + dot(left_bf[span], coef_t[...])
        copy = pltpu.make_async_copy(blend.at[span], out_hbm.at[span], store_sems.at[1 + k])
        copy.start()
        stores.append(copy)
    for number, other in numbers:
        links.wait(number, squares.at[other])
    total = squares[0]
    for i in range(1, nt):
        total = total + squares[i]
    scale = 1.0 / jnp.sqrt(total[0:1, :] + eps_value)
    newb[...] = (coef[...] * scale).astype(bf16)
    newb_copy = pltpu.make_async_copy(newb, newb_hbm, store_sems.at[1 + nx])
    newb_copy.start()
    for copy in links.sent:
        copy.wait_send()
    left_copy.wait()
    for copy in stores:
        copy.wait()
    newb_copy.wait()


def body(dims, momentum, gradient, basis):
    nx, ny, nz = dims
    nt = 2 * nx
    rows, width = momentum.shape
    rank = basis.shape[1]
    share = rows // nt
    half = rank // 2
    fine = NB // nt
    nb = rank // NB
    piece_rows = nb * (nb + 1) // 2 * fine
    v = pltpu.VMEM
    scratch = [
        v((rows, width), f32), v((rows, width), bf16), v((width, rank), bf16),
        v((rows, width), bf16), v((rows, width), bf16),
        v((rows, rank), f32), v((rows // 2, rank), f32),
        v((nx // 2, share, rank), f32), v((nx // 2, share, rank), f32),
        v((rows, rank), f32),
        v((rank, rows), f32), v((rank, rows), bf16), v((rank, rows), bf16),
        v((piece_rows, NB), f32), v((ny - 1, piece_rows // ny, NB), f32), v((nz, piece_rows // ny, NB), f32),
        v((8, 128), f32), v((nt, piece_rows, NB), f32),
        v((rank, rank), f32), v((rank, rank), f32), v((NB, 2 * NB), f32), v((NB, NB), f32), v((rank, rank), f32),
        v((rank, width), f32),
        v((ny // 2, half // ny, width), f32), v((ny // 2, half // ny, width), f32),
        v((nz // 2, half // ny // nz, width), f32), v((nz // 2, half // ny // nz, width), f32),
        v((nz // 2, half // nz, width), f32), v((nz // 2, half // nz, width), f32),
        v((ny // 2, half // ny // nz, width), f32), v((ny // 2, half // ny // nz, width), f32),
        v((rank, width), f32),
        v((rank, width), bf16), v((width, rank), f32), v((nt, 8, rank), f32),
        v((rows, rank), bf16), v((share, rank), f32), v((width, rank), bf16),
        pltpu.SemaphoreType.DMA((2 * nx + 1,)), pltpu.SemaphoreType.DMA((nx + 2,)),
        pltpu.SemaphoreType.DMA((128,)), pltpu.SemaphoreType.DMA((128,)),
    ]
    hbm = pl.BlockSpec(memory_space=pl.ANY)
    return pl.pallas_call(
        functools.partial(kernel, dims),
        out_shape=(
            jax.ShapeDtypeStruct((rows, width), f32),
            jax.ShapeDtypeStruct((share, rank), f32),
            jax.ShapeDtypeStruct((width, rank), bf16),
        ),
        in_specs=[hbm, hbm, hbm],
        out_specs=(hbm, hbm, hbm),
        scratch_shapes=scratch,
        compiler_params=pltpu.CompilerParams(
            collective_id=0, has_side_effects=True, vmem_limit_bytes=56 * 2**20
        ),
    )(momentum, gradient, basis)


def solution(mesh):
    dims = (4, 4, 8)
    placed = (P("fsdp", "tensor"), P("fsdp", "tensor"), P("tensor", None))
    return jax.shard_map(
        functools.partial(body, dims),
        mesh=mesh,
        in_specs=placed,
        out_specs=(P("fsdp", "tensor"), P(("fsdp", "tensor"), None), P("tensor", None)),
        check_vma=False,
    )
```

time: 615 us -> 140 us (0.23)
  waiting for transfers between devices: 366 us -> 0 us
  Pallas kernels: 0 us -> 133 us
  other arithmetic: 128 us -> 0 us
  matrix products: 61.5 us -> 0 us
  blocking collectives: 17.2 us -> 0 us
  between operations: 16.9 us -> 0.66 us
  local copies, waits for them, and re-layouts: 19.6 us -> 6.14 us
    psum x3 -> x0, waiting for transfers between devices: 366 us -> none  [the longest x1 148 us: right_side(): coefficients = lax.psum(partial_coef, 'fsdp')]
    pallas_call x0 -> x1, Pallas kernels: none -> 133 us  [body(): pl.pallas_call(functools.partial(kernel, dims), out_shape=(jax.ShapeDtype...]
    another operation x18 -> x0, other arithmetic: 125 us -> none  [the longest x14 80.7 us: body(): factor_low = jnp.linalg.cholesky(gram)]
    dot_general x4 -> x0, matrix products: 42 us -> none  [the longest x2 19.7 us: dense_tn(): lax.dot_general(left_mat, right_mat, (((0,), (0,)), ((), ())), precision=...]
    another operation x13 -> x0, matrix products: 19.5 us -> none  [the longest x7 11.7 us: solve_right(): lax.linalg.triangular_solve(factor_low, matrix, left_side=False, lower=Tr...]
    psum x1 -> x0, blocking collectives: 17.2 us -> none  [right_side(): squares = lax.psum(jnp.sum(coefficients * coefficients, axis=0), 'tensor')]
    another operation x17 -> x0, local copies, waits for them, and re-layouts: 12.3 us -> none
  transfers between devices with their start and end apart: 3 -> 0, of which waited for: 3 -> 0; matrix products, arithmetic and copies ran while one was open for 1% -> 0% of each run, Pallas kernels for 0% -> 0%
where the time goes in v1:
time: 140 us
  Pallas kernels  133 us (95%)
  local copies, waits for them, and re-layouts  6.14 us (4%)
    pallas_call x1, Pallas kernels, body(): pl.pallas_call(functools.partial(kernel, dims), out_shape=(jax.ShapeDtype...  133 us
    unnamed x7, local copies, waits for them, and re-layouts  6.14 us

profile of v1, /device:TPU:1, one launch (start us, length us, event | category | flops | bytes accessed | tf_op | source)
XLA Modules:
  0.0 139.6 jit_solution(4760779058537862178)
XLA Ops:
  0.6 132.8 %shard_map.58 = (f32[896,1024]{1,0:T(8,128)}, f32[112,512]{1,0:T(8,128)}, bf16[1024,512]{1,0:T(8,128)(2,1)}) custom-call(f32[896,1024]{1,0:T(8,128)} %mom_hbm.1, bf16[896,1024]{1,0:T(8,128)(2,1)} %grad_hbm.1, bf16[1024,512]{1,0:T(8,128)(2,1)} %basis_hbm.1), custom_call_target="tpu_custom_call" | custom-call | tf_op jit(solution)/shard_map/pallas_call | solution.py:502
  133.4 0.0 copy-start.1
  133.5 0.0 copy-start
  133.5 4.5 %copy.9 = f32[896,1024]{1,0:T(8,128)} copy(f32[896,1024]{1,0:T(8,128)} %get-tuple-element.6) | data formatting | bytes 7340032
  137.9 0.0 copy-done.1
  137.9 0.7 copy.10
  138.6 0.0 copy-done
  138.6 1.0 copy.11
Async XLA Ops:
  133.4 4.5 %copy-start.1 = (f32[112,512]{1,0:T(8,128)S(1)}, f32[112,512]{1,0:T(8,128)}, u32[]{:S(2)}) copy-start(f32[112,512]{1,0:T(8,128)} %get-tuple-element.7) | copy-start | bytes 688132
  133.5 5.2 %copy-start = (bf16[1024,512]{1,0:T(8,128)(2,1)S(1)}, bf16[1024,512]{1,0:T(8,128)(2,1)}, u32[]{:S(2)}) copy-start(bf16[1024,512]{1,0:T(8,128)(2,1)} %get-tuple-element.8) | copy-start | bytes 3145732

commit v2 on v1

v2 whole, which is shorter than its diff:
```python
import functools

import jax
import jax.numpy as jnp
from jax import lax
from jax.experimental import pallas as pl
from jax.experimental.pallas import tpu as pltpu
from jax.sharding import PartitionSpec as P

mu_value = 0.95
eps_value = 1e-06
f32 = jnp.float32
bf16 = jnp.bfloat16
MESH = pl.DeviceIdType.MESH
HIGHEST = lax.Precision.HIGHEST
NB = 128

RING_CHUNKS = (1, 2)
PLAN = (
    "p0", "p1", "p2", "p3", "p0", "p1", "p2", "p3", "p0", "p0", "p1", "w0", "p1", "p2", "w1", "p2",
    "p3", "w2", "p3", "g", "w3", "w0", "w1", "w2", "g", "w0", "w3", "w1", "g", "w2", "w0", "w3",
    "g", "w1", "g", "f", "f", "w2", "f", "f", "w0", "f", "w3", "f", "f", "f", "f", "w1", "f", "f",
    "f", "f", "f", "w2", "f", "f", "f", "f", "f", "f", "w3", "f", "f", "f", "f", "w1", "f", "f",
    "f", "f", "w2", "f", "f", "f", "f", "w1", "f", "f", "f", "f", "w2", "l",
)


def dot(left, right, dims=((1,), (0,)), precision=None):
    return lax.dot_general(left, right, (dims, ((), ())), precision=precision, preferred_element_type=f32)


def exact_dot(left, right, dims=((1,), (0,))):
    return dot(left, right, dims, HIGHEST)


def split2(value):
    high = value.astype(bf16)
    return high, (value - high.astype(f32)).astype(bf16)


def dot3(left, right, dims=((1,), (0,))):
    left_high, left_low = left
    right_high, right_low = right
    return dot(left_high, right_high, dims) + (dot(left_low, right_high, dims) + dot(left_high, right_low, dims))


def factor_groups(work, inverse, first, last):
    for group in range(first, last):
        r0 = 8 * group
        n = NB - r0
        cols = [jnp.broadcast_to(work[r0:NB, r0 + j : r0 + j + 1], (n, 128)) for j in range(8)]
        top = work[r0 : r0 + 8, :]
        rows = []
        for k in range(8):
            inv = lax.rsqrt(cols[k][k : k + 1, :])
            c = cols[k] * inv
            cols[k] = c
            for j in range(k + 1, 8):
                cols[j] = cols[j] - c * c[j : j + 1, :]
            row = top[k : k + 1, :] * jnp.concatenate([inv, inv], axis=1)
            rows.append(row)
            if k < 7:
                top = top - jnp.concatenate([c[0:8], c[0:8]], axis=1) * row
            inverse[r0 + k : r0 + k + 1, :] = row[:, 128:]
        if n > 8:
            for half in (slice(0, 128), slice(128, 256)):
                rest = work[r0 + 8 : NB, half]
                for k in range(8):
                    rest = rest - cols[k][8:] * rows[k][:, half]
                work[r0 + 8 : NB, half] = rest


class Links:
    def __init__(self, dims, send_sems, recv_sems):
        self.nx, self.ny, self.nz = dims
        f, t = lax.axis_index("fsdp"), lax.axis_index("tensor")
        self.y, self.z = f // self.nz, lax.rem(f, self.nz)
        self.x, self.c = t // 2, lax.rem(t, 2)
        self.t, self.f = t, f
        self.send_sems, self.recv_sems = send_sems, recv_sems
        self.count = 0
        self.sent = []

    def size(self, axis):
        return {"x": self.nx, "y": self.ny, "z": self.nz}[axis]

    def pos(self, axis):
        return {"x": self.x, "y": self.y, "z": self.z}[axis]

    def at(self, axis, offset):
        n = self.size(axis)
        return lax.rem(self.pos(axis) + (offset % n), n)

    def device(self, dx=0, dy=0, dz=0, core=0):
        x, y, z = self.at("x", dx), self.at("y", dy), self.at("z", dz)
        c = 1 - self.c if core else self.c
        return (y * self.nz + z, x * 2 + c)

    def along(self, axis, offset):
        return self.device(**{"d" + axis: offset})

    def send(self, src, dst, device):
        number = self.count
        self.count += 1
        copy = pltpu.make_async_remote_copy(
            src_ref=src,
            dst_ref=dst,
            send_sem=self.send_sems.at[number],
            recv_sem=self.recv_sems.at[number],
            device_id=device,
            device_id_type=MESH,
        )
        copy.start()
        self.sent.append(copy)
        return number

    def wait(self, number, landing):
        pltpu.make_async_remote_copy(
            src_ref=landing,
            dst_ref=landing,
            send_sem=self.send_sems.at[number],
            recv_sem=self.recv_sems.at[number],
            device_id=self.device(core=1),
            device_id_type=MESH,
        ).wait_recv()


def cut(view):
    size = view.shape[0]
    return view.at[0 : size // 2], view.at[size // 2 : size]


def reduce_ring(links, axis, block, plus, minus):
    half = links.size(axis) // 2
    state = {}

    def add(target, slot, number):
        links.wait(number, slot)
        target[...] = target[...] + slot[...]

    def step(s):
        k = half + 1 - s
        ahead, behind = block(links.at(axis, k)), block(links.at(axis, -k))
        if s > 1:
            target, slot = (cut(ahead)[0], cut(plus.at[s - 2])[0]) if s == 2 else (ahead, plus.at[s - 2])
            add(target, slot, state["plus"])
        src, dst = (cut(ahead)[0], cut(plus.at[s - 1])[0]) if s == 1 else (ahead, plus.at[s - 1])
        state["plus"] = links.send(src, dst, links.along(axis, 1))
        if s > 1:
            target, slot = (cut(behind)[1], cut(minus.at[s - 2])[1]) if s == 2 else (behind, minus.at[s - 2])
            add(target, slot, state["minus"])
        src, dst = (cut(behind)[1], cut(minus.at[s - 1])[1]) if s == 1 else (behind, minus.at[s - 1])
        state["minus"] = links.send(src, dst, links.along(axis, -1))

    def last():
        own = block(links.pos(axis))
        target, slot = (cut(own)[0], cut(plus.at[0])[0]) if half == 1 else (own, plus.at[half - 1])
        add(target, slot, state["plus"])
        target, slot = (cut(own)[1], cut(minus.at[0])[1]) if half == 1 else (own, minus.at[half - 1])
        add(target, slot, state["minus"])

    return [functools.partial(step, s) for s in range(1, half + 1)] + [last]


def gather_ring(links, axis, block, on_block=None):
    n = links.size(axis)
    half = n // 2
    state = {}

    def step(s):
        ahead, behind = block(links.at(axis, 1 - s)), block(links.at(axis, s - 1))
        if s > 1:
            links.wait(state["plus"], ahead)
        view = cut(ahead)[0] if s == half else ahead
        state["plus"] = links.send(view, view, links.along(axis, 1))
        if s > 1:
            links.wait(state["minus"], behind)
        view = cut(behind)[1] if s == half else behind
        state["minus"] = links.send(view, view, links.along(axis, -1))
        if on_block is not None:
            on_block(links.at(axis, 1 - s))
            if s > 1:
                on_block(links.at(axis, s - 1))

    def last():
        far = cut(block(links.at(axis, half)))
        links.wait(state["plus"], far[0])
        links.wait(state["minus"], far[1])
        if on_block is not None:
            on_block(links.at(axis, half))

    return [functools.partial(step, s) for s in range(1, half + 1)] + [last]


def scatter_direct(links, axis, block, slots):
    n = links.size(axis)
    numbers = []

    def send():
        for d in range(1, n):
            numbers.append(links.send(block(links.at(axis, d)), slots.at[d - 1], links.along(axis, d)))

    def add():
        own = block(links.pos(axis))
        total = own[...]
        for d, number in zip(range(1, n), numbers):
            links.wait(number, slots.at[d - 1])
            total = total + slots[d - 1]
        own[...] = total

    return send, add


def gather_direct(links, axis, block, on_block=None):
    n = links.size(axis)
    numbers = []

    def send():
        own = block(links.pos(axis))
        for d in range(1, n):
            numbers.append(links.send(own, own, links.along(axis, d)))
        if on_block is not None:
            on_block(links.pos(axis))

    def wait():
        for d, number in zip(range(1, n), numbers):
            links.wait(number, block(links.at(axis, -d)))
            if on_block is not None:
                on_block(links.at(axis, -d))

    return send, wait


def chain(*steps):
    def run():
        for step in steps:
            step()

    return run


def kernel(
    dims,
    mom_hbm, grad_hbm, basis_hbm,
    out_hbm, left_hbm, newb_hbm,
    blend, grad, basis, blend_hi, blend_lo, part, from_core, x_slots,
    full, flip, flip_hi, flip_lo,
    piece, from_y, from_z, tiles, gram_all, sym, low, work, diag_inv, inverse,
    wide, y_slots, y_plus, y_minus, z_slots, wide_all,
    coef_t, coef, squares, left_bf, left_own, newb,
    load_sems, store_sems, send_sems, recv_sems,
):
    nx, ny, nz = dims
    nt = 2 * nx
    rows, width = blend.shape
    rank = basis.shape[1]
    chunk = rank // 4
    share = rows // nt
    links = Links(dims, send_sems, recv_sems)
    chip_rows = 2 * share

    loads = []
    basis_copy = pltpu.make_async_copy(basis_hbm, basis, load_sems.at[2 * nx])
    basis_copy.start()
    for k in range(nx):
        chip = links.at("x", [nx // 2, 1, nx - 1, 0][k] if nx == 4 else k + 1)
        span = pl.ds(pl.multiple_of(chip * chip_rows, chip_rows), chip_rows)
        m = pltpu.make_async_copy(mom_hbm.at[span], blend.at[span], load_sems.at[2 * k])
        g = pltpu.make_async_copy(grad_hbm.at[span], grad.at[span], load_sems.at[2 * k + 1])
        m.start()
        g.start()
        loads.append((m, g, span, chip))

    barrier = pltpu.get_barrier_semaphore()
    peers = [links.device(core=1)]
    peers += [links.device(dx=d, core=c) for d in range(1, nx) for c in (0, 1)]
    peers += [links.along("y", d) for d in range(1, ny)]
    peers += [links.along("z", d) for d in range(1, nz)]
    peers += [links.device(dx=dx, dy=dy) for dx in range(1, nx) for dy in range(1, ny)]
    for peer in peers:
        pl.semaphore_signal(barrier, inc=1, device_id=peer, device_id_type=MESH)

    def share_of(ref, chip, core):
        return ref.at[:, pl.ds(pl.multiple_of((2 * chip + core) * share, share), share)]

    def joined(*pieces):
        return jnp.concatenate(pieces, axis=1)

    basis_copy.wait()
    core_numbers = []
    for m, g, span, chip in loads:
        m.wait()
        g.wait()
        value = blend[span] + grad[span].astype(f32)
        blend[span] = value
        high = value.astype(bf16)
        rest = value - high.astype(f32)
        mid = rest.astype(bf16)
        tail = (rest - mid.astype(f32)).astype(bf16)
        blend_hi[span] = high
        blend_lo[span] = mid
        q = basis[...]
        product = dot(high, q) + (dot(mid, q) + dot(tail, q))
        for j in range(4):
            part[j, span, :] = product[:, j * chunk : (j + 1) * chunk]
        if not core_numbers:
            pl.semaphore_wait(barrier, len(peers))
        number = links.send(
            share_of(part, chip, 1 - links.c), from_core.at[:, pl.ds(chip * share, share)], links.device(core=1)
        )
        core_numbers.append((number, chip))
    for number, chip in core_numbers:
        landing = from_core.at[:, pl.ds(chip * share, share)]
        links.wait(number, landing)
        mine = share_of(part, chip, links.c)
        mine[...] = mine[...] + landing[...]

    nb = rank // NB
    fine = NB // nt

    cols = width // nz

    def rows_of(ref, row, size):
        return ref.at[:, pl.ds(pl.multiple_of(row, 8), size)]

    def tile_of(ref, row, size, i):
        return ref.at[i, pl.ds(pl.multiple_of(row, 8), size)]

    def gather_core(view):
        numbers = []

        def to_core(chip):
            numbers.append((links.send(view(chip, links.c), view(chip, links.c), links.device(core=1)), chip))

        def finish():
            for number, chip in numbers:
                links.wait(number, view(chip, 1 - links.c))

        return to_core, finish

    def project_steps(j):
        cols = slice(j * chunk, (j + 1) * chunk)

        def partial_view(chip):
            return share_of(part, chip, links.c).at[j]

        def full_view(chip, core):
            return share_of(full, chip, core).at[j]

        def keep():
            full_view(links.x, links.c)[...] = partial_view(links.x)[...]

        def turn():
            for i in range(rows // 128):
                block = full[j, 128 * i : 128 * i + 128, :].T
                flip[cols, 128 * i : 128 * i + 128] = block
                high, lower = split2(block)
                flip_hi[cols, 128 * i : 128 * i + 128] = high
                flip_lo[cols, 128 * i : 128 * i + 128] = lower

        send, add = scatter_direct(links, "x", partial_view, x_slots.at[j])
        to_core, finish = gather_core(full_view)
        share_out, wait = gather_direct(links, "x", lambda i: full_view(i, links.c), to_core)
        return [send, chain(add, keep, share_out), wait, chain(finish, turn)]

    def wide_steps(j, ring):
        base, size = j * chunk, chunk // ny
        mine = base + links.y * size
        span = slice(base, base + chunk)

        def multiply():
            for n in range(width // 256):
                part_cols = slice(256 * n, 256 * n + 256)
                values = dot3((flip_hi[span, :], flip_lo[span, :]), (blend_hi[:, part_cols], blend_lo[:, part_cols]))
                for m in range(256 // cols):
                    wide[256 // cols * n + m, span, :] = values[:, cols * m : cols * m + cols]

        def keep():
            tile_of(wide_all, mine, size, links.z)[...] = tile_of(wide, mine, size, links.z)[...]

        z_send, z_add = scatter_direct(links, "z", functools.partial(tile_of, wide, mine, size), z_slots.at[j])
        z_share, z_wait = gather_direct(links, "z", functools.partial(tile_of, wide_all, mine, size))
        middle = chain(z_add, keep, z_share)

        def y_block(ref, i):
            return rows_of(ref, base + i * size, size)

        if ring:
            out = reduce_ring(links, "y", functools.partial(y_block, wide), y_plus.at[j], y_minus.at[j])
            back = gather_ring(links, "y", functools.partial(y_block, wide_all))
            return (
                [chain(multiply, out[0])] + out[1:-1] + [chain(out[-1], z_send), middle, chain(z_wait, back[0])]
                + back[1:]
            )
        y_send, y_add = scatter_direct(links, "y", functools.partial(y_block, wide), y_slots.at[j])
        y_share, y_wait = gather_direct(links, "y", functools.partial(y_block, wide_all))
        return [chain(multiply, y_send), chain(y_add, z_send), middle, chain(z_wait, y_share), y_wait]

    blocks = [(i, j) for i in range(nb) for j in range(i, nb)]
    y_rows = len(blocks) * fine // ny

    def gram_y(ref, i):
        return ref.at[pl.ds(pl.multiple_of(i * y_rows, 8), y_rows)]

    def gram_steps():
        gy_send, gy_add = scatter_direct(links, "y", functools.partial(gram_y, piece), from_y)
        gz_send, gz_wait = gather_direct(links, "z", lambda i: from_z.at[i])
        to_core, finish = gather_core(lambda chip, core: gram_all.at[2 * chip + core])
        numbers = {}

        def strip():
            picked = jnp.concatenate(
                [flip[pl.ds(pl.multiple_of(NB * i + fine * links.t, 8), fine), :] for i in range(nb)], axis=0
            )
            values = joined(*[exact_dot(picked, joined(full[j], full[j + 1])) for j in (0, 2)])
            for b, (i, j) in enumerate(blocks):
                piece[b * fine : b * fine + fine, :] = values[i * fine : i * fine + fine, NB * j : NB * j + NB]
            gy_send()

        def along_z():
            gy_add()
            from_z[links.z] = gram_y(piece, links.y)[...]
            gz_send()

        def along_xy():
            gz_wait()
            total = from_z[0]
            for i in range(1, nz):
                total = total + from_z[i]
            mine = gram_y(gram_all.at[links.t], links.y)
            mine[...] = total
            for dx in range(nx):
                for dy in range(ny):
                    if dx or dy:
                        numbers[dx, dy] = links.send(mine, mine, links.device(dx=dx, dy=dy))

        def wait_xy():
            for dx in range(nx):
                chip = links.at("x", -dx)
                for dy in range(ny):
                    if dx or dy:
                        links.wait(numbers[dx, dy], gram_y(gram_all.at[2 * chip + links.c], links.at("y", -dy)))
                to_core(chip)

        def assemble():
            finish()
            for b, (i, j) in enumerate(blocks):
                for s in range(nt):
                    sym[NB * i + fine * s : NB * i + fine * s + fine, NB * j : NB * j + NB] = gram_all[
                        s, b * fine : b * fine + fine, :
                    ]

        return [strip, along_z, along_xy, wait_xy, assemble]

    def factor():
        eye = jnp.where(
            lax.broadcasted_iota(jnp.int32, (NB, NB), 0) == lax.broadcasted_iota(jnp.int32, (NB, NB), 1), 1.0, 0.0
        ).astype(f32)
        low[...] = jnp.zeros_like(low)
        inverse[...] = jnp.zeros_like(inverse)
        for k in range(nb):
            s = slice(NB * k, NB * k + NB)
            work[:, :NB] = sym[s, s]
            work[:, NB:] = eye
            for g in range(0, 16, 2):
                factor_groups(work, diag_inv, g, g + 2)
                yield
            block_inv = diag_inv[...]
            inverse[s, s] = block_inv
            if k:
                inverse[s, 0 : NB * k] = exact_dot(block_inv, low[s, 0 : NB * k])
            if k < nb - 1:
                upper = exact_dot(block_inv, sym[s, NB * k + NB :])
                for i in range(k + 1, nb):
                    column = upper[:, NB * (i - k - 1) : NB * (i - k)]
                    sym[NB * i : NB * i + NB, NB * i :] -= exact_dot(
                        column, upper[:, NB * (i - k - 1) :], ((0,), (0,))
                    )
                low[NB * k + NB :, 0 : NB * k + NB] -= exact_dot(upper, inverse[s, 0 : NB * k + NB], ((0,), (0,)))
            yield

    stores = []

    def left():
        inverse_parts = split2(inverse[...])
        mine = share_of(full, links.x, links.c)
        left_own[...] = exact_dot(joined(*[mine[j] for j in range(4)]), inverse[...], ((1,), (1,)))
        copy = pltpu.make_async_copy(left_own, left_hbm, store_sems.at[0])
        copy.start()
        stores.append(copy)
        for k in range(nx):
            span = slice(k * chip_rows, (k + 1) * chip_rows)
            values = split2(joined(*[full[j, span, :] for j in range(4)]))
            left_bf[span] = dot3(values, inverse_parts, ((1,), (1,))).astype(bf16)

    work_lists = {"g": gram_steps(), "l": [left], "f": factor()}
    for j in range(4):
        work_lists["p%d" % j] = project_steps(j)
        work_lists["w%d" % j] = wide_steps(j, j in RING_CHUNKS)
    for name in PLAN:
        if name == "f":
            next(work_lists["f"])
        else:
            work_lists[name].pop(0)()
    assert not any(work_lists[name] for name in work_lists if name != "f")
    assert next(work_lists["f"], None) is None
    inverse_parts = split2(inverse[...])
    lanes = cols
    for j in range(width // 256):
        cols = slice(256 * j, 256 * j + 256)
        block = dot3(inverse_parts, split2(joined(*[wide_all[256 // lanes * j + m] for m in range(256 // lanes)])))
        coef_t[:, cols] = ((mu_value - 1.0) * block).astype(bf16)
        for q in range(2):
            for r in range(rank // 128):
                coef[256 * j + 128 * q : 256 * j + 128 * q + 128, 128 * r : 128 * r + 128] = block[
                    128 * r : 128 * r + 128, 128 * q : 128 * q + 128
                ].T
    value = coef[...]
    mine = squares.at[links.t]
    mine[...] = jnp.broadcast_to(jnp.sum(value * value, axis=0, keepdims=True), (8, rank))
    numbers = []
    for d in range(nx):
        for core in (0, 1):
            if d or core:
                other = 2 * links.at("x", -d) + (1 - links.c if core else links.c)
                numbers.append((links.send(mine, mine, links.device(dx=d, core=core)), other))
    for k in range(nx):
        span = slice(k * chip_rows, (k + 1) * chip_rows)
        blend[span] = blend[span] + dot(left_bf[span], coef_t[...])
        copy = pltpu.make_async_copy(blend.at[span], out_hbm.at[span], store_sems.at[1 + k])
        copy.start()
        stores.append(copy)
    for number, other in numbers:
        links.wait(number, squares.at[other])
    total = squares[0]
    for i in range(1, nt):
        total = total + squares[i]
    scale = 1.0 / jnp.sqrt(total[0:1, :] + eps_value)
    newb[...] = (coef[...] * scale).astype(bf16)
    newb_copy = pltpu.make_async_copy(newb, newb_hbm, store_sems.at[1 + nx])
    newb_copy.start()
    for copy in links.sent:
        copy.wait_send()
    for copy in stores:
        copy.wait()
    newb_copy.wait()


def body(dims, momentum, gradient, basis):
    nx, ny, nz = dims
    nt = 2 * nx
    rows, width = momentum.shape
    rank = basis.shape[1]
    share = rows // nt
    chunk = rank // 4
    fine = NB // nt
    nb = rank // NB
    piece_rows = nb * (nb + 1) // 2 * fine
    v = pltpu.VMEM
    scratch = [
        v((rows, width), f32), v((rows, width), bf16), v((width, rank), bf16),
        v((rows, width), bf16), v((rows, width), bf16),
        v((4, rows, chunk), f32), v((4, rows // 2, chunk), f32),
        v((4, nx - 1, share, rank // 4), f32),
        v((4, rows, chunk), f32),
        v((rank, rows), f32), v((rank, rows), bf16), v((rank, rows), bf16),
        v((piece_rows, NB), f32), v((ny - 1, piece_rows // ny, NB), f32), v((nz, piece_rows // ny, NB), f32),
        v((8, 128), f32), v((nt, piece_rows, NB), f32),
        v((rank, rank), f32), v((rank, rank), f32), v((NB, 2 * NB), f32), v((NB, NB), f32), v((rank, rank), f32),
        v((nz, rank, width // nz), f32),
        v((4, ny - 1, nz, chunk // ny, width // nz), f32),
        v((4, ny // 2, nz, chunk // ny, width // nz), f32), v((4, ny // 2, nz, chunk // ny, width // nz), f32),
        v((4, nz - 1, chunk // ny, width // nz), f32),
        v((nz, rank, width // nz), f32),
        v((rank, width), bf16), v((width, rank), f32), v((nt, 8, rank), f32),
        v((rows, rank), bf16), v((share, rank), f32), v((width, rank), bf16),
        pltpu.SemaphoreType.DMA((2 * nx + 1,)), pltpu.SemaphoreType.DMA((nx + 2,)),
        pltpu.SemaphoreType.DMA((192,)), pltpu.SemaphoreType.DMA((192,)),
    ]
    hbm = pl.BlockSpec(memory_space=pl.ANY)
    results = pl.pallas_call(
        functools.partial(kernel, dims),
        out_shape=(
            jax.ShapeDtypeStruct((rows, width), f32),
            jax.ShapeDtypeStruct((share, rank), f32),
            jax.ShapeDtypeStruct((width, rank), bf16),
        ),
        in_specs=[hbm, hbm, hbm],
        out_specs=(hbm, hbm, hbm),
        scratch_shapes=scratch,
        compiler_params=pltpu.CompilerParams(
            collective_id=0, has_side_effects=True, vmem_limit_bytes=58 * 2**20
        ),
    )(momentum, gradient, basis)
    return pl.pallas_call(
        hand_over,
        out_shape=tuple(jax.ShapeDtypeStruct(r.shape, r.dtype) for r in results),
        in_specs=[hbm, hbm, hbm],
        out_specs=(hbm, hbm, hbm),
        scratch_shapes=[pltpu.VMEM(r.shape, r.dtype) for r in results] + [pltpu.SemaphoreType.DMA((20,))],
        compiler_params=pltpu.CompilerParams(vmem_limit_bytes=32 * 2**20),
    )(*results)


def hand_over(big, left, newb, big_out, left_out, newb_out, big_v, left_v, newb_v, sems):
    size = big.shape[0] // 8
    parts = [(big.at[pl.ds(size * i, size)], big_v.at[pl.ds(size * i, size)], big_out.at[pl.ds(size * i, size)])
             for i in range(8)]
    parts += [(left, left_v, left_out), (newb, newb_v, newb_out)]
    reads = [pltpu.make_async_copy(src, mid, sems.at[i]) for i, (src, mid, _) in enumerate(parts)]
    writes = [pltpu.make_async_copy(mid, dst, sems.at[10 + i]) for i, (_, mid, dst) in enumerate(parts)]
    for copy in reads:
        copy.start()
    for read, write in zip(reads, writes):
        read.wait()
        write.start()
    for write in writes:
        write.wait()


def solution(mesh):
    dims = (4, 4, 8)
    placed = (P("fsdp", "tensor"), P("fsdp", "tensor"), P("tensor", None))
    return jax.shard_map(
        functools.partial(body, dims),
        mesh=mesh,
        in_specs=placed,
        out_specs=(P("fsdp", "tensor"), P(("fsdp", "tensor"), None), P("tensor", None)),
        check_vma=False,
    )
```

time: 140 us -> 109 us (0.78)
  Pallas kernels: 133 us -> 104 us
  local copies, waits for them, and re-layouts: 6.14 us -> 4.19 us
    pallas_call x1, Pallas kernels: 133 us -> 98.7 us  [body(): pl.pallas_call(functools.partial(kernel, dims), out_shape=(jax.ShapeDtype...]
    pallas_call x0 -> x1, Pallas kernels: none -> 4.95 us  [body(): pl.pallas_call(hand_over, out_shape=tuple((jax.ShapeDtypeStruct(r.shape,...]
    unnamed x7 -> x6, local copies, waits for them, and re-layouts: 6.14 us -> 4.19 us
where the time goes in v2:
time: 109 us
  Pallas kernels  104 us (95%)
  local copies, waits for them, and re-layouts  4.19 us (4%)
    pallas_call x1, Pallas kernels, body(): pl.pallas_call(functools.partial(kernel, dims), out_shape=(jax.ShapeDtype...  98.7 us
    pallas_call x1, Pallas kernels, body(): pl.pallas_call(hand_over, out_shape=tuple((jax.ShapeDtypeStruct(r.shape,...  4.95 us
    unnamed x6, local copies, waits for them, and re-layouts  4.19 us

profile of v2, /device:TPU:1, one launch (start us, length us, event | category | flops | bytes accessed | tf_op | source)
XLA Modules:
  0.0 108.7 jit_solution(12974976710615339433)
XLA Ops:
  0.6 98.7 %shard_map.58 = (f32[896,1024]{1,0:T(8,128)}, f32[112,512]{1,0:T(8,128)}, bf16[1024,512]{1,0:T(8,128)(2,1)}) custom-call(f32[896,1024]{1,0:T(8,128)} %mom_hbm.1, bf16[896,1024]{1,0:T(8,128)(2,1)} %grad_hbm.1, bf16[1024,512]{1,0:T(8,128)(2,1)} %basis_hbm.1), custom_call_target="tpu_custom_call" | custom-call | tf_op jit(solution)/shard_map/pallas_call | solution.py:581
  99.3 0.0 copy-start
  99.4 2.0 %copy-done = f32[896,1024]{1,0:T(8,128)S(1)} copy-done((f32[896,1024]{1,0:T(8,128)S(1)}, f32[896,1024]{1,0:T(8,128)}, u32[]{:S(2)}) %copy-start) | copy-done | bytes 3670040
  101.4 0.0 copy-start.1
  101.4 1.2 %copy-done.1 = bf16[1024,512]{1,0:T(8,128)(2,1)S(1)} copy-done((bf16[1024,512]{1,0:T(8,128)(2,1)S(1)}, bf16[1024,512]{1,0:T(8,128)(2,1)}, u32[]{:S(2)}) %copy-start.1) | copy-done | bytes 1048600
  102.6 0.0 copy-start.2
  102.6 0.9 copy-done.2
  103.5 5.0 %shard_map.59 = (f32[896,1024]{1,0:T(8,128)}, f32[112,512]{1,0:T(8,128)}, bf16[1024,512]{1,0:T(8,128)(2,1)}) custom-call(f32[896,1024]{1,0:T(8,128)S(1)} %copy-done, f32[112,512]{1,0:T(8,128)S(1)} %copy-done.2, bf16[1024,512]{1,0:T(8,128)(2,1)S(1)} %copy-done.1), custom_call_target="tpu_custom_call" | custom-call | tf_op jit(solution)/shard_map/pallas_call | solution.py:595
Async XLA Ops:
  99.3 2.0 %copy-start = (f32[896,1024]{1,0:T(8,128)S(1)}, f32[896,1024]{1,0:T(8,128)}, u32[]{:S(2)}) copy-start(f32[896,1024]{1,0:T(8,128)} %get-tuple-element.6.big) | copy-start | bytes 11010052
  101.4 1.2 %copy-start.1 = (bf16[1024,512]{1,0:T(8,128)(2,1)S(1)}, bf16[1024,512]{1,0:T(8,128)(2,1)}, u32[]{:S(2)}) copy-start(bf16[1024,512]{1,0:T(8,128)(2,1)} %get-tuple-element.8.newb) | copy-start | bytes 3145732
  102.6 0.9 copy-start.2

commit v3 on v2

--- a/solution.py
+++ b/solution.py
@@ -15,13 +15,14 @@
 HIGHEST = lax.Precision.HIGHEST
 NB = 128
 
-RING_CHUNKS = (1, 2)
+KINDS = ('C', 'A1', 'C', 'C')
 PLAN = (
-    "p0", "p1", "p2", "p3", "p0", "p1", "p2", "p3", "p0", "p0", "p1", "w0", "p1", "p2", "w1", "p2",
-    "p3", "w2", "p3", "g", "w3", "w0", "w1", "w2", "g", "w0", "w3", "w1", "g", "w2", "w0", "w3",
-    "g", "w1", "g", "f", "f", "w2", "f", "f", "w0", "f", "w3", "f", "f", "f", "f", "w1", "f", "f",
-    "f", "f", "f", "w2", "f", "f", "f", "f", "f", "f", "w3", "f", "f", "f", "f", "w1", "f", "f",
-    "f", "f", "w2", "f", "f", "f", "f", "w1", "f", "f", "f", "f", "w2", "l",
+    "p0", "p1", "p2", "p3", "p0", "p1", "p2", "p3", "p0", "p0", "p1", "w0", "p1", "ga", "p2", "w1",
+    "p3", "p2", "w2", "p3", "gb", "ga", "w0", "w3", "w2", "w1", "gb", "ga", "w3", "w0", "w2", "ga",
+    "w1", "ga", "w3", "gb", "f", "f", "w0", "f", "f", "w2", "f", "f", "f", "f", "w1", "f", "w3",
+    "f", "gb", "f", "w0", "f", "f", "gb", "w2", "f", "f", "f", "f", "f", "w3", "f", "w1", "f", "f",
+    "f", "w0", "f", "f", "f", "f", "w2", "f", "f", "f", "f", "w3", "f", "f", "w0", "f", "f", "f",
+    "f", "w2", "l", "w3",
 )
 
 
@@ -192,38 +193,38 @@
     return [functools.partial(step, s) for s in range(1, half + 1)] + [last]
 
 
-def scatter_direct(links, axis, block, slots):
-    n = links.size(axis)
+def scatter_direct(links, axis, block, slots, stride=1):
+    offsets = range(stride, links.size(axis), stride)
     numbers = []
 
     def send():
-        for d in range(1, n):
-            numbers.append(links.send(block(links.at(axis, d)), slots.at[d - 1], links.along(axis, d)))
+        for i, d in enumerate(offsets):
+            numbers.append(links.send(block(links.at(axis, d)), slots.at[i], links.along(axis, d)))
 
     def add():
         own = block(links.pos(axis))
         total = own[...]
-        for d, number in zip(range(1, n), numbers):
-            links.wait(number, slots.at[d - 1])
-            total = total + slots[d - 1]
+        for i, number in enumerate(numbers):
+            links.wait(number, slots.at[i])
+            total = total + slots[i]
         own[...] = total
 
     return send, add
 
 
-def gather_direct(links, axis, block, on_block=None):
-    n = links.size(axis)
+def gather_direct(links, axis, block, on_block=None, stride=1):
+    offsets = range(stride, links.size(axis), stride)
     numbers = []
 
     def send():
         own = block(links.pos(axis))
-        for d in range(1, n):
+        for d in offsets:
             numbers.append(links.send(own, own, links.along(axis, d)))
         if on_block is not None:
             on_block(links.pos(axis))
 
     def wait():
-        for d, number in zip(range(1, n), numbers):
+        for d, number in zip(offsets, numbers):
             links.wait(number, block(links.at(axis, -d)))
             if on_block is not None:
                 on_block(links.at(axis, -d))
@@ -245,8 +246,8 @@
     out_hbm, left_hbm, newb_hbm,
     blend, grad, basis, blend_hi, blend_lo, part, from_core, x_slots,
     full, flip, flip_hi, flip_lo,
-    piece, from_y, from_z, tiles, gram_all, sym, low, work, diag_inv, inverse,
-    wide, y_slots, y_plus, y_minus, z_slots, wide_all,
+    piece_a, from_y_a, from_z_a, gram_a, piece_b, from_y_b, from_z_b, gram_b, sym, low, work, diag_inv, inverse,
+    wide, y_slots, y_plus, y_minus, z_slots, pair_slots, wide_all,
     coef_t, coef, squares, left_bf, left_own, newb,
     load_sems, store_sems, send_sems, recv_sems,
 ):
@@ -321,10 +322,16 @@
     cols = width // nz
 
     def rows_of(ref, row, size):
-        return ref.at[:, pl.ds(pl.multiple_of(row, 8), size)]
+        return ref.at[:, :, pl.ds(pl.multiple_of(row, 8), size)]
 
     def tile_of(ref, row, size, i):
-        return ref.at[i, pl.ds(pl.multiple_of(row, 8), size)]
+        return ref.at[lax.rem(i, 2), i // 2, pl.ds(pl.multiple_of(row, 8), size)]
+
+    parity = lax.rem(links.z, 2)
+    turn_z = 1 - 2 * parity
+    pair_devices = [
+        (links.y * nz + lax.rem(links.z + nz + sign * turn_z, nz), links.t) for sign in (1, -1)
+    ]
 
     def gather_core(view):
         numbers = []
@@ -363,7 +370,7 @@
         share_out, wait = gather_direct(links, "x", lambda i: full_view(i, links.c), to_core)
         return [send, chain(add, keep, share_out), wait, chain(finish, turn)]
 
-    def wide_steps(j, ring):
+    def wide_steps(j, kind):
         base, size = j * chunk, chunk // ny
         mine = base + links.y * size
         span = slice(base, base + chunk)
@@ -373,7 +380,8 @@
                 part_cols = slice(256 * n, 256 * n + 256)
                 values = dot3((flip_hi[span, :], flip_lo[span, :]), (blend_hi[:, part_cols], blend_lo[:, part_cols]))
                 for m in range(256 // cols):
-                    wide[256 // cols * n + m, span, :] = values[:, cols * m : cols * m + cols]
+                    tile = 256 // cols * n + m
+                    wide[tile % 2, tile // 2, span, :] = values[:, cols * m : cols * m + cols]
 
         def keep():
             tile_of(wide_all, mine, size, links.z)[...] = tile_of(wide, mine, size, links.z)[...]
@@ -385,7 +393,45 @@
         def y_block(ref, i):
             return rows_of(ref, base + i * size, size)
 
-        if ring:
+        if kind == "C":
+            numbers = []
+
+            def side(ref, which, h):
+                return ref.at[which, :, base + h * (chunk // 2) : base + (h + 1) * (chunk // 2)]
+
+            def pair_send():
+                for h in (0, 1):
+                    numbers.append(links.send(side(wide, 1 - parity, h), pair_slots.at[j, h], pair_devices[h]))
+
+            def pair_add():
+                for h in (0, 1):
+                    links.wait(numbers[h], pair_slots.at[j, h])
+                    mine_side = side(wide, parity, h)
+                    mine_side[...] = mine_side[...] + pair_slots[j, h]
+
+            def pair_share():
+                for h in (0, 1):
+                    view = side(wide_all, parity, h)
+                    numbers.append(links.send(view, view, pair_devices[h]))
+
+            def pair_wait():
+                for h in (0, 1):
+                    links.wait(numbers[2 + h], side(wide_all, 1 - parity, h))
+
+            def half_block(ref, i):
+                return ref.at[parity, :, pl.ds(pl.multiple_of(base + i * size, 8), size)]
+
+            y_send, y_add = scatter_direct(links, "y", functools.partial(half_block, wide), y_slots.at[j, :, 0])
+            y_share, y_wait = gather_direct(links, "y", functools.partial(half_block, wide_all))
+            z_send, z_add = scatter_direct(
+                links, "z", functools.partial(tile_of, wide, mine, size), z_slots.at[j], 2
+            )
+            z_share, z_wait = gather_direct(links, "z", functools.partial(tile_of, wide_all, mine, size), None, 2)
+            return [
+                chain(multiply, pair_send), chain(pair_add, y_send), chain(y_add, z_send),
+                chain(z_add, keep, z_share), chain(z_wait, y_share), chain(y_wait, pair_share), pair_wait,
+            ]
+        if kind == "A2":
             out = reduce_ring(links, "y", functools.partial(y_block, wide), y_plus.at[j], y_minus.at[j])
             back = gather_ring(links, "y", functools.partial(y_block, wide_all))
             return (
@@ -396,30 +442,31 @@
         y_share, y_wait = gather_direct(links, "y", functools.partial(y_block, wide_all))
         return [chain(multiply, y_send), chain(y_add, z_send), middle, chain(z_wait, y_share), y_wait]
 
-    blocks = [(i, j) for i in range(nb) for j in range(i, nb)]
-    y_rows = len(blocks) * fine // ny
-
-    def gram_y(ref, i):
-        return ref.at[pl.ds(pl.multiple_of(i * y_rows, 8), y_rows)]
-
-    def gram_steps():
-        gy_send, gy_add = scatter_direct(links, "y", functools.partial(gram_y, piece), from_y)
+    def gram_steps(first_col, row_blocks, piece, from_y, from_z, gathered):
+        y_rows = piece.shape[0] // ny
+        tiles = [(i, j) for i in range(row_blocks) for j in (first_col, first_col + 1)]
+
+        def y_part(ref, i):
+            return ref.at[pl.ds(pl.multiple_of(i * y_rows, 8), y_rows)]
+
+        gy_send, gy_add = scatter_direct(links, "y", functools.partial(y_part, piece), from_y)
         gz_send, gz_wait = gather_direct(links, "z", lambda i: from_z.at[i])
-        to_core, finish = gather_core(lambda chip, core: gram_all.at[2 * chip + core])
+        to_core, finish = gather_core(lambda chip, core: gathered.at[2 * chip + core])
         numbers = {}
 
         def strip():
             picked = jnp.concatenate(
-                [flip[pl.ds(pl.multiple_of(NB * i + fine * links.t, 8), fine), :] for i in range(nb)], axis=0
+                [flip[pl.ds(pl.multiple_of(NB * i + fine * links.t, 8), fine), :] for i in range(row_blocks)], axis=0
             )
-            values = joined(*[exact_dot(picked, joined(full[j], full[j + 1])) for j in (0, 2)])
-            for b, (i, j) in enumerate(blocks):
-                piece[b * fine : b * fine + fine, :] = values[i * fine : i * fine + fine, NB * j : NB * j + NB]
+            values = exact_dot(picked, joined(full[first_col], full[first_col + 1]))
+            for b, (i, j) in enumerate(tiles):
+                c = NB * (j - first_col)
+                piece[b * fine : b * fine + fine, :] = values[i * fine : i * fine + fine, c : c + NB]
             gy_send()
 
         def along_z():
             gy_add()
-            from_z[links.z] = gram_y(piece, links.y)[...]
+            from_z[links.z] = y_part(piece, links.y)[...]
             gz_send()
 
         def along_xy():
@@ -427,7 +474,7 @@
             total = from_z[0]
             for i in range(1, nz):
                 total = total + from_z[i]
-            mine = gram_y(gram_all.at[links.t], links.y)
+            mine = y_part(gathered.at[links.t], links.y)
             mine[...] = total
             for dx in range(nx):
                 for dy in range(ny):
@@ -439,14 +486,14 @@
                 chip = links.at("x", -dx)
                 for dy in range(ny):
                     if dx or dy:
-                        links.wait(numbers[dx, dy], gram_y(gram_all.at[2 * chip + links.c], links.at("y", -dy)))
+                        links.wait(numbers[dx, dy], y_part(gathered.at[2 * chip + links.c], links.at("y", -dy)))
                 to_core(chip)
 
         def assemble():
             finish()
-            for b, (i, j) in enumerate(blocks):
+            for b, (i, j) in enumerate(tiles):
                 for s in range(nt):
-                    sym[NB * i + fine * s : NB * i + fine * s + fine, NB * j : NB * j + NB] = gram_all[
+                    sym[NB * i + fine * s : NB * i + fine * s + fine, NB * j : NB * j + NB] = gathered[
                         s, b * fine : b * fine + fine, :
                     ]
 
@@ -456,10 +503,15 @@
         eye = jnp.where(
             lax.broadcasted_iota(jnp.int32, (NB, NB), 0) == lax.broadcasted_iota(jnp.int32, (NB, NB), 1), 1.0, 0.0
         ).astype(f32)
+        inverse[...] = jnp.zeros_like(inverse)
         low[...] = jnp.zeros_like(low)
-        inverse[...] = jnp.zeros_like(inverse)
+        top, rest = slice(0, 2 * NB), slice(2 * NB, rank)
         for k in range(nb):
             s = slice(NB * k, NB * k + NB)
+            if k == 2:
+                upper = exact_dot(inverse[top, top], sym[top, rest])
+                sym[rest, rest] -= exact_dot(upper, upper, ((0,), (0,)))
+                low[rest, top] = -exact_dot(upper, inverse[top, top], ((0,), (0,)))
             work[:, :NB] = sym[s, s]
             work[:, NB:] = eye
             for g in range(0, 16, 2):
@@ -469,14 +521,11 @@
             inverse[s, s] = block_inv
             if k:
                 inverse[s, 0 : NB * k] = exact_dot(block_inv, low[s, 0 : NB * k])
-            if k < nb - 1:
-                upper = exact_dot(block_inv, sym[s, NB * k + NB :])
-                for i in range(k + 1, nb):
-                    column = upper[:, NB * (i - k - 1) : NB * (i - k)]
-                    sym[NB * i : NB * i + NB, NB * i :] -= exact_dot(
-                        column, upper[:, NB * (i - k - 1) :], ((0,), (0,))
-                    )
-                low[NB * k + NB :, 0 : NB * k + NB] -= exact_dot(upper, inverse[s, 0 : NB * k + NB], ((0,), (0,)))
+            if k % 2 == 0:
+                after = slice(NB * k + NB, NB * k + 2 * NB)
+                upper = exact_dot(block_inv, sym[s, after])
+                sym[after, after] -= exact_dot(upper, upper, ((0,), (0,)))
+                low[after, 0 : NB * k + NB] -= exact_dot(upper, inverse[s, 0 : NB * k + NB], ((0,), (0,)))
             yield
 
     stores = []
@@ -493,10 +542,15 @@
             values = split2(joined(*[full[j, span, :] for j in range(4)]))
             left_bf[span] = dot3(values, inverse_parts, ((1,), (1,))).astype(bf16)
 
-    work_lists = {"g": gram_steps(), "l": [left], "f": factor()}
+    work_lists = {
+        "ga": gram_steps(0, nb // 2, piece_a, from_y_a, from_z_a, gram_a),
+        "gb": gram_steps(nb // 2, nb, piece_b, from_y_b, from_z_b, gram_b),
+        "l": [left],
+        "f": factor(),
+    }
     for j in range(4):
         work_lists["p%d" % j] = project_steps(j)
-        work_lists["w%d" % j] = wide_steps(j, j in RING_CHUNKS)
+        work_lists["w%d" % j] = wide_steps(j, KINDS[j])
     for name in PLAN:
         if name == "f":
             next(work_lists["f"])
@@ -508,7 +562,7 @@
     lanes = cols
     for j in range(width // 256):
         cols = slice(256 * j, 256 * j + 256)
-        block = dot3(inverse_parts, split2(joined(*[wide_all[256 // lanes * j + m] for m in range(256 // lanes)])))
+        block = dot3(inverse_parts, split2(joined(*[wide_all[i % 2, i // 2] for i in range(256 // lanes * j, 256 // lanes * (j + 1))])))
         coef_t[:, cols] = ((mu_value - 1.0) * block).astype(bf16)
         for q in range(2):
             for r in range(rank // 128):
@@ -554,9 +608,13 @@
     share = rows // nt
     chunk = rank // 4
     fine = NB // nt
-    nb = rank // NB
-    piece_rows = nb * (nb + 1) // 2 * fine
     v = pltpu.VMEM
+
+    def gram_scratch(size):
+        return (
+            v((size, NB), f32), v((ny - 1, size // ny, NB), f32), v((nz, size // ny, NB), f32), v((nt, size, NB), f32)
+        )
+
     scratch = [
         v((rows, width), f32), v((rows, width), bf16), v((width, rank), bf16),
         v((rows, width), bf16), v((rows, width), bf16),
@@ -564,18 +622,18 @@
         v((4, nx - 1, share, rank // 4), f32),
         v((4, rows, chunk), f32),
         v((rank, rows), f32), v((rank, rows), bf16), v((rank, rows), bf16),
-        v((piece_rows, NB), f32), v((ny - 1, piece_rows // ny, NB), f32), v((nz, piece_rows // ny, NB), f32),
-        v((8, 128), f32), v((nt, piece_rows, NB), f32),
+        *gram_scratch(4 * fine), *gram_scratch(8 * fine),
         v((rank, rank), f32), v((rank, rank), f32), v((NB, 2 * NB), f32), v((NB, NB), f32), v((rank, rank), f32),
-        v((nz, rank, width // nz), f32),
-        v((4, ny - 1, nz, chunk // ny, width // nz), f32),
-        v((4, ny // 2, nz, chunk // ny, width // nz), f32), v((4, ny // 2, nz, chunk // ny, width // nz), f32),
-        v((4, nz - 1, chunk // ny, width // nz), f32),
-        v((nz, rank, width // nz), f32),
+        v((2, nz // 2, rank, width // nz), f32),
+        v((4, ny - 1, 2, nz // 2, chunk // ny, width // nz), f32),
+        v((4, ny // 2, 2, nz // 2, chunk // ny, width // nz), f32),
+        v((4, ny // 2, 2, nz // 2, chunk // ny, width // nz), f32),
+        v((4, nz - 1, chunk // ny, width // nz), f32), v((4, 2, nz // 2, chunk // 2, width // nz), f32),
+        v((2, nz // 2, rank, width // nz), f32),
         v((rank, width), bf16), v((width, rank), f32), v((nt, 8, rank), f32),
         v((rows, rank), bf16), v((share, rank), f32), v((width, rank), bf16),
         pltpu.SemaphoreType.DMA((2 * nx + 1,)), pltpu.SemaphoreType.DMA((nx + 2,)),
-        pltpu.SemaphoreType.DMA((192,)), pltpu.SemaphoreType.DMA((192,)),
+        pltpu.SemaphoreType.DMA((224,)), pltpu.SemaphoreType.DMA((224,)),
     ]
     hbm = pl.BlockSpec(memory_space=pl.ANY)
     results = pl.pallas_call(
@@ -598,7 +656,7 @@
         in_specs=[hbm, hbm, hbm],
         out_specs=(hbm, hbm, hbm),
         scratch_shapes=[pltpu.VMEM(r.shape, r.dtype) for r in results] + [pltpu.SemaphoreType.DMA((20,))],
-        compiler_params=pltpu.CompilerParams(vmem_limit_bytes=32 * 2**20),
+        compiler_params=pltpu.CompilerParams(vmem_limit_bytes=62 * 2**20),
     )(*results)
 
 

time: 109 us -> 99.9 us (0.917)
  Pallas kernels: 104 us -> 99 us
  local copies, waits for them, and re-layouts: 4.19 us -> 0 us
    pallas_call x1, Pallas kernels: 98.7 us -> 94.3 us  [body(): pl.pallas_call(functools.partial(kernel, dims), out_shape=(jax.ShapeDtype...]
    unnamed x6 -> x0, local copies, waits for them, and re-layouts: 4.19 us -> none
where the time goes in v3:
time: 99.9 us; the launch traced here: 99.8 us
  Pallas kernels  99 us (99%)
    pallas_call x1, Pallas kernels, body(): pl.pallas_call(functools.partial(kernel, dims), out_shape=(jax.ShapeDtype...  94.3 us
    pallas_call x1, Pallas kernels, body(): pl.pallas_call(hand_over, out_shape=tuple((jax.ShapeDtypeStruct(r.shape,...  4.69 us

profile of v3, /device:TPU:1, one launch (start us, length us, event | category | flops | bytes accessed | tf_op | source)
XLA Modules:
  0.0 99.8 jit_solution(6489365063071412390)
XLA Ops:
  0.6 94.3 %shard_map.58 = (f32[896,1024]{1,0:T(8,128)}, f32[112,512]{1,0:T(8,128)}, bf16[1024,512]{1,0:T(8,128)(2,1)}) custom-call(f32[896,1024]{1,0:T(8,128)} %mom_hbm.1, bf16[896,1024]{1,0:T(8,128)(2,1)} %grad_hbm.1, bf16[1024,512]{1,0:T(8,128)(2,1)} %basis_hbm.1), custom_call_target="tpu_custom_call" | custom-call | tf_op jit(solution)/shard_map/pallas_call | solution.py:639
  94.9 4.7 %shard_map.59 = (f32[896,1024]{1,0:T(8,128)}, f32[112,512]{1,0:T(8,128)}, bf16[1024,512]{1,0:T(8,128)(2,1)}) custom-call(f32[896,1024]{1,0:T(8,128)} %get-tuple-element.6.big, f32[112,512]{1,0:T(8,128)} %get-tuple-element.7.left, bf16[1024,512]{1,0:T(8,128)(2,1)} %get-tuple-element.8.newb), custom_call_target="tpu_custom_call" | custom-call | tf_op jit(solution)/shard_map/pallas_call | solution.py:653

commit v4 on v3

--- a/solution.py
+++ b/solution.py
@@ -15,14 +15,14 @@
 HIGHEST = lax.Precision.HIGHEST
 NB = 128
 
-KINDS = ('C', 'A1', 'C', 'C')
+KINDS = ('C', 'A2', 'C', 'C')
 PLAN = (
-    "p0", "p1", "p2", "p3", "p0", "p1", "p2", "p3", "p0", "p0", "p1", "w0", "p1", "ga", "p2", "w1",
-    "p3", "p2", "w2", "p3", "gb", "ga", "w0", "w3", "w2", "w1", "gb", "ga", "w3", "w0", "w2", "ga",
-    "w1", "ga", "w3", "gb", "f", "f", "w0", "f", "f", "w2", "f", "f", "f", "f", "w1", "f", "w3",
-    "f", "gb", "f", "w0", "f", "f", "gb", "w2", "f", "f", "f", "f", "f", "w3", "f", "w1", "f", "f",
-    "f", "w0", "f", "f", "f", "f", "w2", "f", "f", "f", "f", "w3", "f", "f", "w0", "f", "f", "f",
-    "f", "w2", "l", "w3",
+    "p0", "p1", "p2", "p3", "p0", "p1", "p2", "p3", "p0", "p0", "w0", "p1", "p2", "p1", "ga", "w1",
+    "p2", "p3", "w2", "w0", "p3", "gb", "ga", "w3", "w1", "w2", "w0", "gb", "ga", "w1", "w3", "w0",
+    "w2", "ga", "gb", "ga", "w3", "f", "f", "w1", "f", "f", "w0", "f", "f", "w2", "f", "f", "f",
+    "gb", "f", "w3", "f", "f", "f", "gb", "w1", "f", "w0", "f", "w2", "f", "f", "f", "f", "w3", "f",
+    "f", "w1", "f", "w0", "f", "f", "f", "f", "w2", "f", "f", "l", "f", "f", "l", "w3", "f", "w1",
+    "f", "l", "f", "f", "l", "f", "w2", "f", "l", "w3",
 )
 
 
@@ -248,7 +248,7 @@
     full, flip, flip_hi, flip_lo,
     piece_a, from_y_a, from_z_a, gram_a, piece_b, from_y_b, from_z_b, gram_b, sym, low, work, diag_inv, inverse,
     wide, y_slots, y_plus, y_minus, z_slots, pair_slots, wide_all,
-    coef_t, coef, squares, left_bf, left_own, newb,
+    coef_wide, coef_t, coef, squares, left_bf, left_own, newb,
     load_sems, store_sems, send_sems, recv_sems,
 ):
     nx, ny, nz = dims
@@ -530,22 +530,26 @@
 
     stores = []
 
-    def left():
-        inverse_parts = split2(inverse[...])
+    def left_columns(first, last, k):
+        span, cols_out = slice(k * chip_rows, (k + 1) * chip_rows), slice(first, last)
+        values = split2(joined(*[full[j, span, :] for j in range(last // chunk)]))
+        left_bf[span, cols_out] = dot3(values, split2(inverse[cols_out, 0:last]), ((1,), (1,))).astype(bf16)
+
+    def left_last():
+        for k in range(nx):
+            left_columns(3 * NB, rank, k)
+
+    def left_rows():
         mine = share_of(full, links.x, links.c)
         left_own[...] = exact_dot(joined(*[mine[j] for j in range(4)]), inverse[...], ((1,), (1,)))
         copy = pltpu.make_async_copy(left_own, left_hbm, store_sems.at[0])
         copy.start()
         stores.append(copy)
-        for k in range(nx):
-            span = slice(k * chip_rows, (k + 1) * chip_rows)
-            values = split2(joined(*[full[j, span, :] for j in range(4)]))
-            left_bf[span] = dot3(values, inverse_parts, ((1,), (1,))).astype(bf16)
 
     work_lists = {
         "ga": gram_steps(0, nb // 2, piece_a, from_y_a, from_z_a, gram_a),
         "gb": gram_steps(nb // 2, nb, piece_b, from_y_b, from_z_b, gram_b),
-        "l": [left],
+        "l": [functools.partial(left_columns, 0, 3 * NB, k) for k in range(nx)] + [left_last],
         "f": factor(),
     }
     for j in range(4):
@@ -559,19 +563,20 @@
     assert not any(work_lists[name] for name in work_lists if name != "f")
     assert next(work_lists["f"], None) is None
     inverse_parts = split2(inverse[...])
-    lanes = cols
+    square_sum = jnp.zeros((rank, cols), f32)
     for j in range(width // 256):
-        cols = slice(256 * j, 256 * j + 256)
-        block = dot3(inverse_parts, split2(joined(*[wide_all[i % 2, i // 2] for i in range(256 // lanes * j, 256 // lanes * (j + 1))])))
-        coef_t[:, cols] = ((mu_value - 1.0) * block).astype(bf16)
-        for q in range(2):
-            for r in range(rank // 128):
-                coef[256 * j + 128 * q : 256 * j + 128 * q + 128, 128 * r : 128 * r + 128] = block[
-                    128 * r : 128 * r + 128, 128 * q : 128 * q + 128
-                ].T
-    value = coef[...]
+        wide_cols = joined(*[wide_all[i % 2, i // 2] for i in range(256 // cols * j, 256 // cols * (j + 1))])
+        block = dot3(inverse_parts, split2(wide_cols))
+        out_cols = slice(256 * j, 256 * j + 256)
+        coef_wide[:, out_cols] = block
+        coef_t[:, out_cols] = ((mu_value - 1.0) * block).astype(bf16)
+        for m in range(256 // cols):
+            tile = block[:, m * cols : (m + 1) * cols]
+            square_sum = square_sum + tile * tile
     mine = squares.at[links.t]
-    mine[...] = jnp.broadcast_to(jnp.sum(value * value, axis=0, keepdims=True), (8, rank))
+    for r in range(nb):
+        span = slice(NB * r, NB * r + NB)
+        mine[:, span] = jnp.broadcast_to(jnp.sum(square_sum[span, :].T, axis=0, keepdims=True), (8, NB))
     numbers = []
     for d in range(nx):
         for core in (0, 1):
@@ -584,6 +589,12 @@
         copy = pltpu.make_async_copy(blend.at[span], out_hbm.at[span], store_sems.at[1 + k])
         copy.start()
         stores.append(copy)
+    left_rows()
+    for j in range(width // 128):
+        for r in range(nb):
+            coef[128 * j : 128 * j + 128, NB * r : NB * r + NB] = coef_wide[
+                NB * r : NB * r + NB, 128 * j : 128 * j + 128
+            ].T
     for number, other in numbers:
         links.wait(number, squares.at[other])
     total = squares[0]
@@ -630,7 +641,7 @@
         v((4, ny // 2, 2, nz // 2, chunk // ny, width // nz), f32),
         v((4, nz - 1, chunk // ny, width // nz), f32), v((4, 2, nz // 2, chunk // 2, width // nz), f32),
         v((2, nz // 2, rank, width // nz), f32),
-        v((rank, width), bf16), v((width, rank), f32), v((nt, 8, rank), f32),
+        v((rank, width), f32), v((rank, width), bf16), v((width, rank), f32), v((nt, 8, rank), f32),
         v((rows, rank), bf16), v((share, rank), f32), v((width, rank), bf16),
         pltpu.SemaphoreType.DMA((2 * nx + 1,)), pltpu.SemaphoreType.DMA((nx + 2,)),
         pltpu.SemaphoreType.DMA((224,)), pltpu.SemaphoreType.DMA((224,)),

time: 99.9 us -> 96.7 us (0.968)
  Pallas kernels: 99 us -> 95.8 us
    pallas_call x1, Pallas kernels: 94.3 us -> 91.1 us  [body(): pl.pallas_call(functools.partial(kernel, dims), out_shape=(jax.ShapeDtype...]
where the time goes in v4:
time: 96.7 us; the launch traced here: 96.6 us
  Pallas kernels  95.8 us (99%)
    pallas_call x1, Pallas kernels, body(): pl.pallas_call(functools.partial(kernel, dims), out_shape=(jax.ShapeDtype...  91.1 us
    pallas_call x1, Pallas kernels, body(): pl.pallas_call(hand_over, out_shape=tuple((jax.ShapeDtypeStruct(r.shape,...  4.69 us

profile of v4, /device:TPU:1, one launch (start us, length us, event | category | flops | bytes accessed | tf_op | source)
XLA Modules:
  0.0 96.6 jit_solution(13037373271148465793)
XLA Ops:
  0.6 91.1 %shard_map.58 = (f32[896,1024]{1,0:T(8,128)}, f32[112,512]{1,0:T(8,128)}, bf16[1024,512]{1,0:T(8,128)(2,1)}) custom-call(f32[896,1024]{1,0:T(8,128)} %mom_hbm.1, bf16[896,1024]{1,0:T(8,128)(2,1)} %grad_hbm.1, bf16[1024,512]{1,0:T(8,128)(2,1)} %basis_hbm.1), custom_call_target="tpu_custom_call" | custom-call | tf_op jit(solution)/shard_map/pallas_call | solution.py:650
  91.7 4.7 %shard_map.59 = (f32[896,1024]{1,0:T(8,128)}, f32[112,512]{1,0:T(8,128)}, bf16[1024,512]{1,0:T(8,128)(2,1)}) custom-call(f32[896,1024]{1,0:T(8,128)} %get-tuple-element.6.big, f32[112,512]{1,0:T(8,128)} %get-tuple-element.7.left, bf16[1024,512]{1,0:T(8,128)(2,1)} %get-tuple-element.8.newb), custom_call_target="tpu_custom_call" | custom-call | tf_op jit(solution)/shard_map/pallas_call | solution.py:664

commit v5 on v4

--- a/solution.py
+++ b/solution.py
@@ -195,17 +195,18 @@
 
 def scatter_direct(links, axis, block, slots, stride=1):
     offsets = range(stride, links.size(axis), stride)
-    numbers = []
-
-    def send():
+    numbers = {}
+
+    def send(only=None):
         for i, d in enumerate(offsets):
-            numbers.append(links.send(block(links.at(axis, d)), slots.at[i], links.along(axis, d)))
+            if d not in numbers and only in (None, d):
+                numbers[d] = links.send(block(links.at(axis, d)), slots.at[i], links.along(axis, d))
 
     def add():
         own = block(links.pos(axis))
         total = own[...]
-        for i, number in enumerate(numbers):
-            links.wait(number, slots.at[i])
+        for i, d in enumerate(offsets):
+            links.wait(numbers[d], slots.at[i])
             total = total + slots[i]
         own[...] = total
 
@@ -289,6 +290,16 @@
 
     basis_copy.wait()
     core_numbers = []
+    x_sums = [
+        scatter_direct(links, "x", lambda i, j=j: share_of(part, i, links.c).at[j], x_slots.at[j]) for j in range(4)
+    ]
+
+    def add_core(number, chip):
+        landing = from_core.at[:, pl.ds(chip * share, share)]
+        links.wait(number, landing)
+        mine = share_of(part, chip, links.c)
+        mine[...] = mine[...] + landing[...]
+
     for m, g, span, chip in loads:
         m.wait()
         g.wait()
@@ -310,12 +321,12 @@
             share_of(part, chip, 1 - links.c), from_core.at[:, pl.ds(chip * share, share)], links.device(core=1)
         )
         core_numbers.append((number, chip))
-    for number, chip in core_numbers:
-        landing = from_core.at[:, pl.ds(chip * share, share)]
-        links.wait(number, landing)
-        mine = share_of(part, chip, links.c)
-        mine[...] = mine[...] + landing[...]
-
+        if len(core_numbers) == 2:
+            add_core(*core_numbers[0])
+            for send, _ in x_sums:
+                send(nx // 2)
+    for number, chip in core_numbers[1:]:
+        add_core(number, chip)
     nb = rank // NB
     fine = NB // nt
 
@@ -365,7 +376,7 @@
                 flip_hi[cols, 128 * i : 128 * i + 128] = high
                 flip_lo[cols, 128 * i : 128 * i + 128] = lower
 
-        send, add = scatter_direct(links, "x", partial_view, x_slots.at[j])
+        send, add = x_sums[j]
         to_core, finish = gather_core(full_view)
         share_out, wait = gather_direct(links, "x", lambda i: full_view(i, links.c), to_core)
         return [send, chain(add, keep, share_out), wait, chain(finish, turn)]

time: 96.7 us -> 94.2 us (0.974)
  Pallas kernels: 95.8 us -> 93.3 us
    pallas_call x1, Pallas kernels: 91.1 us -> 88.6 us  [body(): pl.pallas_call(functools.partial(kernel, dims), out_shape=(jax.ShapeDtype...]
where the time goes in v5:
time: 94.2 us; the launch traced here: 94.1 us
  Pallas kernels  93.3 us (99%)
    pallas_call x1, Pallas kernels, body(): pl.pallas_call(functools.partial(kernel, dims), out_shape=(jax.ShapeDtype...  88.6 us
    pallas_call x1, Pallas kernels, body(): pl.pallas_call(hand_over, out_shape=tuple((jax.ShapeDtypeStruct(r.shape,...  4.69 us

profile of v5, /device:TPU:1, one launch (start us, length us, event | category | flops | bytes accessed | tf_op | source)
XLA Modules:
  0.0 94.1 jit_solution(3050505788947411755)
XLA Ops:
  0.6 88.6 %shard_map.58 = (f32[896,1024]{1,0:T(8,128)}, f32[112,512]{1,0:T(8,128)}, bf16[1024,512]{1,0:T(8,128)(2,1)}) custom-call(f32[896,1024]{1,0:T(8,128)} %mom_hbm.1, bf16[896,1024]{1,0:T(8,128)(2,1)} %grad_hbm.1, bf16[1024,512]{1,0:T(8,128)(2,1)} %basis_hbm.1), custom_call_target="tpu_custom_call" | custom-call | tf_op jit(solution)/shard_map/pallas_call | solution.py:661
  89.2 4.7 %shard_map.59 = (f32[896,1024]{1,0:T(8,128)}, f32[112,512]{1,0:T(8,128)}, bf16[1024,512]{1,0:T(8,128)(2,1)}) custom-call(f32[896,1024]{1,0:T(8,128)} %get-tuple-element.6.big, f32[112,512]{1,0:T(8,128)} %get-tuple-element.7.left, bf16[1024,512]{1,0:T(8,128)(2,1)} %get-tuple-element.8.newb), custom_call_target="tpu_custom_call" | custom-call | tf_op jit(solution)/shard_map/pallas_call | solution.py:675
